TPU v7x, 32 devices: a whole 2x2x4 slice. The times are simulated.
32 devices in a mesh: groups: 2 (over y), replica: 1, da: 4 (over x, core), db: 4 (over z).
Axes of the slice: x: 2, y: 2, z: 4, core: 2. Of those that a mesh axis runs over, the one named last changes fastest.
Arguments:
- tokens: bfloat16 [4096, 1024], P(('groups', 'replica', 'da', 'db')), parts along dimension 0, may hold values from -6 to 6
- grad_out: bfloat16 [4096, 1024], P(('groups', 'replica', 'da', 'db')), parts along dimension 0, may hold values from -3 to 3
- routes: int32 [4096, 8], P(('groups', 'replica', 'da', 'db')), parts along dimension 0, may hold values from 0 to 15, as said below
- gates: bfloat16 [4096, 8], P(('groups', 'replica', 'da', 'db')), parts along dimension 0, may hold values from 0.019897461 to 0.5
- w_gate_up: bfloat16 [16, 1024, 768], P(('da', 'db'), 'replica'), may hold values from -0.1875 to 0.1875
- w_down: bfloat16 [16, 384, 1024], P(('da', 'db'), 'replica'), may hold values from -0.3125 to 0.3125
Outputs:
- token_grads: bfloat16 [4096, 1024], P(('groups', 'replica', 'da', 'db')), parts along dimension 0
- gate_grads: bfloat16 [4096, 8], P(('groups', 'replica', 'da', 'db')), parts along dimension 0
- gate_up_grads: bfloat16 [32, 1024, 768], P(('groups', 'da', 'db'), 'replica'), parts along dimension 0
- down_grads: bfloat16 [32, 384, 1024], P(('groups', 'da', 'db'), 'replica'), parts along dimension 0
There are 2 independent parts, one for each index of `groups`. A program takes and returns all parts, laid end to end along the dimension named above; an argument that names none is the same for every part. Nothing has to cross between parts.
Inputs may be any that keep to these rules, and one draw needn't show every extreme that they name: `routes`: each token names 8 different experts. In every aligned block of 2 consecutive tokens, each expert is named exactly once, so the tokens of one device name every expert exactly 64 times.
All inputs are finite; a program needn't handle non-finite values.
Results may differ from a plain program's by a relative error of at most 0.0085.
Values may be sent and summed in bfloat16 or wider, within the bound.
No kernel may reach another device: no remote copies, remote signals or barrier semaphores. Data moves between devices by JAX's collectives and lax.ppermute only.
A program may use at most 64 MiB of HBM per device.

v0:
```python
import jax
import jax.numpy as jnp
from jax import lax
from jax.sharding import PartitionSpec as P


def silu_parts(projected):
    sigmoid = jax.nn.sigmoid(projected)
    return (projected * sigmoid, sigmoid * (1.0 + projected * (1.0 - sigmoid)))


def body(tokens, grad_out, routes, gates, w_gate_up, w_down):
    local_tokens, features = tokens.shape
    top_count = routes.shape[1]
    hidden_units = w_gate_up.shape[2] // 2
    first_size = lax.axis_size("da")
    second_size = lax.axis_size("db")
    experts = first_size * second_size
    per_round = experts // top_count
    rounds = local_tokens // per_round
    expert_ids = lax.broadcasted_iota(jnp.int32, (1, 1, 1, experts), 3)
    matches = routes.reshape(rounds, per_round, top_count, 1) == expert_ids
    gate_values = gates.reshape(rounds, per_round, top_count, 1).astype(jnp.float32)
    gate_table = jnp.sum(jnp.where(matches, gate_values, 0.0), axis=(1, 2)).astype(jnp.bfloat16)
    chosen = jnp.any(matches, axis=2).astype(jnp.bfloat16)
    input_send = jnp.einsum(
        "rge,rgd->red",
        chosen,
        tokens.reshape(rounds, per_round, features),
        preferred_element_type=jnp.float32,
    ).astype(jnp.bfloat16)
    upstream_send = jnp.einsum(
        "rge,rgd->red",
        chosen,
        grad_out.reshape(rounds, per_round, features),
        preferred_element_type=jnp.float32,
    ).astype(jnp.bfloat16)
    input_recv, upstream_recv, gate_recv = (
        lax.all_to_all(input_send, ("da", "db"), split_axis=1, concat_axis=1, tiled=True),
        lax.all_to_all(upstream_send, ("da", "db"), split_axis=1, concat_axis=1, tiled=True),
        lax.all_to_all(gate_table, ("da", "db"), split_axis=1, concat_axis=1, tiled=True),
    )
    input_rows = input_recv.reshape(-1, features)
    upstream_rows = upstream_recv.reshape(-1, features)
    gate_rows = gate_recv.reshape(-1, 1).astype(jnp.float32)
    w_in, w_out = (
        lax.all_gather(w_gate_up[0], "replica", axis=0, tiled=True),
        lax.all_gather(w_down[0], "replica", axis=0, tiled=True),
    )
    projected = jnp.dot(input_rows, w_in, preferred_element_type=jnp.float32)
    back_raw = jnp.einsum("rd,fd->rf", upstream_rows, w_out, preferred_element_type=jnp.float32)
    gate_part = projected[:, :hidden_units]
    up_part = projected[:, hidden_units:]
    activated, derivative = silu_parts(gate_part)
    hidden = (activated * up_part).astype(jnp.bfloat16)
    gate_scores = jnp.sum(hidden.astype(jnp.float32) * back_raw, axis=1).astype(jnp.bfloat16)
    back_hidden = gate_rows * back_raw
    grad_projected = jnp.concatenate(
        [back_hidden * up_part * derivative, back_hidden * activated], axis=1
    ).astype(jnp.bfloat16)
    scaled_upstream = (gate_rows * upstream_rows.astype(jnp.float32)).astype(jnp.bfloat16)
    input_grads = jnp.einsum("rf,df->rd", grad_projected, w_in, preferred_element_type=jnp.float32)
    input_grads = input_grads.astype(jnp.bfloat16).reshape(rounds, experts, features)
    score_back = gate_scores.reshape(rounds, experts)
    returned, score_ret = (
        lax.all_to_all(input_grads, ("da", "db"), split_axis=1, concat_axis=1, tiled=True),
        lax.all_to_all(score_back, ("da", "db"), split_axis=1, concat_axis=1, tiled=True),
    )
    score_ret = score_ret.reshape(rounds, 1, 1, experts).astype(jnp.float32)
    token_grads = (
        jnp.einsum("rge,red->rgd", chosen, returned, preferred_element_type=jnp.float32)
        .astype(jnp.bfloat16)
        .reshape(local_tokens, features)
    )
    gate_grads = (
        jnp.sum(jnp.where(matches, score_ret, 0.0), axis=3)
        .astype(jnp.bfloat16)
        .reshape(local_tokens, top_count)
    )
    columns = input_rows
    grad_in = lax.psum_scatter(
        jnp.einsum("rd,rf->df", columns, grad_projected, preferred_element_type=jnp.float32).astype(
            jnp.bfloat16
        ),
        "replica",
        scatter_dimension=0,
        tiled=True,
    )
    columns = hidden
    grad_down = lax.psum_scatter(
        jnp.einsum(
            "rf,rd->fd", columns, scaled_upstream, preferred_element_type=jnp.float32
        ).astype(jnp.bfloat16),
        "replica",
        scatter_dimension=0,
        tiled=True,
    )
    return (token_grads, gate_grads, grad_in[None], grad_down[None])


def solution(mesh):
    placed = (
        P(("groups", "replica", "da", "db"), None),
        P(("groups", "replica", "da", "db"), None),
        P(("groups", "replica", "da", "db"), None),
        P(("groups", "replica", "da", "db"), None),
        P(("da", "db"), "replica", None),
        P(("da", "db"), "replica", None),
    )
    return jax.shard_map(
        body,
        mesh=mesh,
        in_specs=placed,
        out_specs=(
            P(("groups", "replica", "da", "db"), None),
            P(("groups", "replica", "da", "db"), None),
            P(("groups", "da", "db"), "replica", None),
            P(("groups", "da", "db"), "replica", None),
        ),
        check_vma=False,
    )
```

profile of v0, /device:TPU:0, one launch (start us, length us, event | category | flops | bytes accessed | tf_op | source)
XLA Modules:
  0.0 206.7 jit_solution(12314356661567460310)
XLA Ops:
  0.6 0.9 copy.56
  1.8 1.1 reshape.88
  3.6 2.5 %copy.67 = bf16[64,16,1024]{2,0,1:T(8,128)(2,1)} copy(bf16[64,16,1024]{2,1,0:T(8,128)(2,1)S(1)} %convolution_convert_fusion) | data formatting | bytes 4194304 | tf_op jit(solution)/shard_map/convert_element_type | solution.py:31
  6.1 7.5 %all-to-all-start.2 = ((bf16[64,16,1024]{2,0,1:T(8,128)(2,1)}), bf16[64,16,1024]{2,0,1:T(8,128)(2,1)}, u32[]{:S(2)}, u32[]{:S(2)}) async-start(bf16[64,16,1024]{2,0,1:T(8,128)(2,1)} %copy.67), calls=%async_computation.2 | async-start | bytes 4194304 | tf_op jit(solution)/shard_map/all_to_all | solution.py:39
  14.6 2.5 %copy.64 = bf16[64,16,1024]{2,0,1:T(8,128)(2,1)} copy(bf16[64,16,1024]{2,1,0:T(8,128)(2,1)S(1)} %convolution_convert_fusion.1) | data formatting | bytes 4194304 | tf_op jit(solution)/shard_map/convert_element_type | solution.py:37
  17.1 46.1 %all-to-all-done.2 = bf16[64,16,1024]{2,0,1:T(8,128)(2,1)} async-done(((bf16[64,16,1024]{2,0,1:T(8,128)(2,1)}), bf16[64,16,1024]{2,0,1:T(8,128)(2,1)}, u32[]{:S(2)}, u32[]{:S(2)}) %all-to-all-start.2) | async-done | bytes 2097184 | tf_op jit(solution)/shard_map/all_to_all | solution.py:39
  63.1 4.4 %all-to-all-start.1 = ((bf16[64,16,1024]{2,0,1:T(8,128)(2,1)}), bf16[64,16,1024]{2,0,1:T(8,128)(2,1)}, u32[]{:S(2)}, u32[]{:S(2)}) async-start(bf16[64,16,1024]{2,0,1:T(8,128)(2,1)} %copy.64), calls=%async_computation.1 | async-start | bytes 4194304 | tf_op jit(solution)/shard_map/all_to_all | solution.py:40
  67.6 2.7 %copy.68 = bf16[64,16,1024]{2,1,0:T(8,128)(2,1)S(1)} copy(bf16[64,16,1024]{2,0,1:T(8,128)(2,1)} %all-to-all-done.2) | data formatting | bytes 4194304 | tf_op jit(solution)/shard_map/all_to_all | solution.py:39
  70.4 1.4 copy-done.2
  71.7 3.5 %fusion.5 = f32[1024,768]{0,1:T(8,128)} fusion(bf16[1024,1024]{1,0:T(8,128)(2,1)S(1)} %bitcast.35, bf16[1,1024,768]{2,1,0:T(8,128)(2,1)S(1)} %copy-done), kind=kOutput, calls=%fused_computation.11 | convolution fusion | flops 1610612736 | bytes 6815744 | tf_op jit(solution)/shard_map/dot_general | solution.py:50
  75.2 41.8 %all-to-all-done.1 = bf16[64,16,1024]{2,0,1:T(8,128)(2,1)} async-done(((bf16[64,16,1024]{2,0,1:T(8,128)(2,1)}), bf16[64,16,1024]{2,0,1:T(8,128)(2,1)}, u32[]{:S(2)}, u32[]{:S(2)}) %all-to-all-start.1) | async-done | bytes 2097184 | tf_op jit(solution)/shard_map/all_to_all | solution.py:40
  117.0 2.9 %copy.65 = bf16[64,16,1024]{2,1,0:T(8,128)(2,1)S(1)} copy(bf16[64,16,1024]{2,0,1:T(8,128)(2,1)} %all-to-all-done.1) | data formatting | bytes 4194304 | tf_op jit(solution)/shard_map/all_to_all | solution.py:40
  120.0 2.1 multiply_reduce_fusion
  122.8 3.5 %all-to-all-start.4 = ((bf16[64,16,1]{0,2,1:T(2,128)(2,1)}), bf16[64,16,1]{0,2,1:T(2,128)(2,1)S(1)}, u32[]{:S(2)}, u32[]{:S(2)}) async-start(bf16[64,16,1]{0,2,1:T(2,128)(2,1)} %copy.72), calls=%async_computation.4 | async-start | bytes 16384 | tf_op jit(solution)/shard_map/all_to_all | solution.py:67
  126.5 6.1 %all-to-all-done.4 = bf16[64,16,1]{0,2,1:T(2,128)(2,1)S(1)} async-done(((bf16[64,16,1]{0,2,1:T(2,128)(2,1)}), bf16[64,16,1]{0,2,1:T(2,128)(2,1)S(1)}, u32[]{:S(2)}, u32[]{:S(2)}) %all-to-all-start.4) | async-done | bytes 2080 | tf_op jit(solution)/shard_map/all_to_all | solution.py:67
  132.6 8.9 %all_to_all.27 = bf16[64,16,1]{0,2,1:T(2,128)(2,1)S(1)} all-to-all(bf16[64,16,1]{0,2,1:T(2,128)(2,1)S(1)} %copy.60), channel_id=1, replica_groups=mesh['groups'=2,'replica'=1,'da'=4,'db'=4] {'da','db'}, dimensions={1} | all-to-all | bytes 4096 | tf_op jit(solution)/shard_map/all_to_all | solution.py:41
  141.7 2.8 %multiply_convert_fusion.4 = (bf16[1024,384]{0,1:T(8,128)(2,1)S(1)}, bf16[1024,384]{0,1:T(8,128)(2,1)S(1)}) fusion(f32[1024,768]{0,1:T(8,128)} %fusion.5, f32[1024,384]{0,1:T(8,128)S(1)} %get-tuple-element.30, f32[1024]{0:T(1024)S(1)} %reshape.93), kind=kLoop, calls=%fused_computation.16 | loop fusion | flops 5505024 | bytes 6295552 | tf_op jit(solution)/shard_map/convert.3
  144.6 1.8 convolution_convert_fusion.2
  146.4 2.5 %copy.69 = bf16[64,16,1024]{2,0,1:T(8,128)(2,1)} copy(bf16[64,16,1024]{2,1,0:T(8,128)(2,1)S(1)} %bitcast.39) | data formatting | bytes 4194304 | tf_op jit(solution)/shard_map/reshape | solution.py:63
  149.0 4.6 %all-to-all-start.3 = ((bf16[64,16,1024]{2,0,1:T(8,128)(2,1)}), bf16[64,16,1024]{2,0,1:T(8,128)(2,1)}, u32[]{:S(2)}, u32[]{:S(2)}) async-start(bf16[64,16,1024]{2,0,1:T(8,128)(2,1)} %copy.69), calls=%async_computation.3 | async-start | bytes 4194304 | tf_op jit(solution)/shard_map/all_to_all | solution.py:66
  154.3 3.7 %fusion.10 = bf16[1,384,1024]{2,1,0:T(8,128)(2,1)} fusion(bf16[1024,384]{0,1:T(8,128)(2,1)S(1)} %copy-done.12, bf16[1024,1024]{1,0:T(8,128)(2,1)} %bitcast.38, f32[1024]{0:T(1024)S(1)} %reshape.93), kind=kOutput, calls=%fused_computation.21 | convolution fusion | flops 808845312 | bytes 3674112 | tf_op jit(solution)/shard_map/rf,rd->fd/dot_general | solution.py:91
  158.0 3.0 %fusion.8 = bf16[1,1024,768]{2,1,0:T(8,128)(2,1)} fusion(bf16[1024,1024]{1,0:T(8,128)(2,1)S(1)} %bitcast.36, bf16[1024,384]{0,1:T(8,128)(2,1)S(1)} %copy-done.8, bf16[1024,384]{0,1:T(8,128)(2,1)S(1)} %copy-done.6), kind=kOutput, calls=%fused_computation.19 | convolution fusion | flops 1614544896 | bytes 5242880 | tf_op jit(solution)/shard_map/rd,rf->df/dot_general | solution.py:82
  161.0 42.0 %all-to-all-done.3 = bf16[64,16,1024]{2,0,1:T(8,128)(2,1)} async-done(((bf16[64,16,1024]{2,0,1:T(8,128)(2,1)}), bf16[64,16,1024]{2,0,1:T(8,128)(2,1)}, u32[]{:S(2)}, u32[]{:S(2)}) %all-to-all-start.3) | async-done | bytes 2097184 | tf_op jit(solution)/shard_map/all_to_all | solution.py:66
  203.0 2.9 %fusion.11 = bf16[64,2,1024]{2,1,0:T(2,128)(2,1)S(1)} fusion(pred[64,2,16]{2,1,0:T(4,128)(4,1)S(1)} %copy.70, bf16[64,16,1024]{2,0,1:T(8,128)(2,1)} %all-to-all-done.3), kind=kOutput, calls=%fused_computation.22 | convolution fusion | flops 4325376 | bytes 2361344 | tf_op jit(solution)/shard_map/rge,red->rgd/dot_general | solution.py:71
  (44 shorter events, 4.7 us)
Async XLA Ops:
  0.6 71.1 %copy-start = (bf16[1,1024,768]{2,1,0:T(8,128)(2,1)S(1)}, bf16[1,1024,768]{2,1,0:T(8,128)(2,1)}, u32[]{:S(2)}) copy-start(bf16[1,1024,768]{2,1,0:T(8,128)(2,1)} %param.10) | copy-start | bytes 4718596
  6.1 7.6 %copy-start.9 = (bf16[128,1024]{1,0:T(8,128)(2,1)S(1)}, bf16[128,1024]{1,0:T(8,128)(2,1)}, u32[]{:S(2)}) copy-start(bf16[128,1024]{1,0:T(8,128)(2,1)} %param.7) | copy-start | bytes 786436
  6.1 57.0 %all-to-all-start.2 = ((bf16[64,16,1024]{2,0,1:T(8,128)(2,1)}), bf16[64,16,1024]{2,0,1:T(8,128)(2,1)}, u32[]{:S(2)}, u32[]{:S(2)}) async-start(bf16[64,16,1024]{2,0,1:T(8,128)(2,1)} %copy.67), calls=%async_computation.2 | async-start | bytes 4194304 | tf_op jit(solution)/shard_map/all_to_all | solution.py:39
  63.1 53.9 %all-to-all-start.1 = ((bf16[64,16,1024]{2,0,1:T(8,128)(2,1)}), bf16[64,16,1024]{2,0,1:T(8,128)(2,1)}, u32[]{:S(2)}, u32[]{:S(2)}) async-start(bf16[64,16,1024]{2,0,1:T(8,128)(2,1)} %copy.64), calls=%async_computation.1 | async-start | bytes 4194304 | tf_op jit(solution)/shard_map/all_to_all | solution.py:40
  70.3 1.4 copy-start.2
  117.0 2.9 %copy-start.1 = (f32[1024,768]{0,1:T(8,128)S(1)}, f32[1024,768]{0,1:T(8,128)}, u32[]{:S(2)}) copy-start(f32[1024,768]{0,1:T(8,128)} %fusion.5) | copy-start | bytes 9437188
  117.0 2.9 %copy-start.11 = (bf16[1,384,1024]{2,1,0:T(8,128)(2,1)S(1)}, bf16[1,384,1024]{2,1,0:T(8,128)(2,1)}, u32[]{:S(2)}) copy-start(bf16[1,384,1024]{2,1,0:T(8,128)(2,1)} %param.11) | copy-start | bytes 2359300
  119.9 2.1 %copy-start.4 = (bf16[64,16,1024]{2,1,0:T(8,128)(2,1)}, bf16[64,16,1024]{2,1,0:T(8,128)(2,1)S(1)}, u32[]{:S(2)}) copy-start(bf16[64,16,1024]{2,1,0:T(8,128)(2,1)S(1)} %copy.65) | copy-start | bytes 6291460
  120.0 6.3 %copy-start.10 = (bf16[128,8]{0,1:T(8,128)(2,1)S(1)}, bf16[128,8]{0,1:T(8,128)(2,1)}, u32[]{:S(2)}) copy-start(bf16[128,8]{0,1:T(8,128)(2,1)} %param.9) | copy-start | bytes 6148
  122.8 9.7 %all-to-all-start.4 = ((bf16[64,16,1]{0,2,1:T(2,128)(2,1)}), bf16[64,16,1]{0,2,1:T(2,128)(2,1)S(1)}, u32[]{:S(2)}, u32[]{:S(2)}) async-start(bf16[64,16,1]{0,2,1:T(2,128)(2,1)} %copy.72), calls=%async_computation.4 | async-start | bytes 16384 | tf_op jit(solution)/shard_map/all_to_all | solution.py:67
  144.5 1.9 copy-start.5
  144.6 1.9 copy-start.7
  149.0 5.3 %copy-start.12 = (bf16[1024,384]{0,1:T(8,128)(2,1)S(1)}, bf16[1024,384]{0,1:T(8,128)(2,1)}, u32[]{:S(2)}) copy-start(bf16[1024,384]{0,1:T(8,128)(2,1)} %get-tuple-element.27) | copy-start | bytes 2359300
  149.0 54.0 %all-to-all-start.3 = ((bf16[64,16,1024]{2,0,1:T(8,128)(2,1)}), bf16[64,16,1024]{2,0,1:T(8,128)(2,1)}, u32[]{:S(2)}, u32[]{:S(2)}) async-start(bf16[64,16,1024]{2,0,1:T(8,128)(2,1)} %copy.69), calls=%async_computation.3 | async-start | bytes 4194304 | tf_op jit(solution)/shard_map/all_to_all | solution.py:66
  154.3 3.7 %copy-start.3 = (bf16[64,16,1024]{2,1,0:T(8,128)(2,1)S(1)}, bf16[64,16,1024]{2,1,0:T(8,128)(2,1)}, u32[]{:S(2)}) copy-start(bf16[64,16,1024]{2,1,0:T(8,128)(2,1)} %copy-done.2) | copy-start | bytes 6291460
  154.3 3.7 %copy-start.6 = (bf16[1024,384]{0,1:T(8,128)(2,1)S(1)}, bf16[1024,384]{0,1:T(8,128)(2,1)}, u32[]{:S(2)}) copy-start(bf16[1024,384]{0,1:T(8,128)(2,1)} %copy-done.5) | copy-start | bytes 2359300
  154.3 3.7 %copy-start.8 = (bf16[1024,384]{0,1:T(8,128)(2,1)S(1)}, bf16[1024,384]{0,1:T(8,128)(2,1)}, u32[]{:S(2)}) copy-start(bf16[1024,384]{0,1:T(8,128)(2,1)} %copy-done.7) | copy-start | bytes 2359300
where the time goes:
time: 207 us
  waiting for transfers between devices  136 us (66%)
  starting transfers between devices  20 us (10%)
  local copies, waits for them, and re-layouts  19.5 us (9%)
  matrix products  18.6 us (9%)
  blocking collectives  8.93 us (4%)
  other arithmetic  2.92 us (1%)
    all_to_all x1, waiting for transfers between devices, body(): lax.all_to_all(input_send, ('da', 'db'), split_axis=1, concat_axis=1, til...  46.1 us
    all_to_all x1, waiting for transfers between devices, body(): lax.all_to_all(input_grads, ('da', 'db'), split_axis=1, concat_axis=1, ti...  42 us
    all_to_all x1, waiting for transfers between devices, body(): lax.all_to_all(upstream_send, ('da', 'db'), split_axis=1, concat_axis=1,...  41.8 us
    all_to_all x1, blocking collectives, body(): lax.all_to_all(gate_table, ('da', 'db'), split_axis=1, concat_axis=1, til...  8.93 us
    all_to_all x1, starting transfers between devices, body(): lax.all_to_all(input_send, ('da', 'db'), split_axis=1, concat_axis=1, til...  7.54 us
    all_to_all x1, waiting for transfers between devices, body(): lax.all_to_all(score_back, ('da', 'db'), split_axis=1, concat_axis=1, til...  6.05 us
    all_to_all x1, starting transfers between devices, body(): lax.all_to_all(input_grads, ('da', 'db'), split_axis=1, concat_axis=1, ti...  4.57 us
    all_to_all x1, starting transfers between devices, body(): lax.all_to_all(upstream_send, ('da', 'db'), split_axis=1, concat_axis=1,...  4.44 us
  transfers between devices with their start and end apart: 4, of which 4 were waited for; matrix products, arithmetic and copies ran while one was open for 8% of the time, Pallas kernels for 0%

commit v1 on v0

--- a/solution.py
+++ b/solution.py
@@ -1,7 +1,16 @@
+import functools
+
 import jax
 import jax.numpy as jnp
 from jax import lax
+from jax.experimental import pallas as pl
+from jax.experimental.pallas import tpu as pltpu
 from jax.sharding import PartitionSpec as P
+
+LANES = 128
+ROWS = 16
+AXES = ("da", "db")
+VMEM_LIMIT = 40 * 1024 * 1024
 
 
 def silu_parts(projected):
@@ -98,6 +107,208 @@
     return (token_grads, gate_grads, grad_in[None], grad_down[None])
 
 
+def dot(a, b, contract):
+    return lax.dot_general(a, b, ((contract[:1], contract[1:]), ((), ())), preferred_element_type=jnp.float32)
+
+
+def one_hot(table, expert, rounds, per_round):
+    experts, count = table.shape
+    rows = lax.broadcasted_iota(jnp.int32, (experts, count), 0)
+    line = jnp.sum(jnp.where(rows == expert, table.astype(jnp.float32), 0.0), axis=0, keepdims=True)
+    token_block = lax.broadcasted_iota(jnp.int32, (rounds, count), 1) // per_round
+    mine = lax.broadcasted_iota(jnp.int32, (rounds, count), 0) == token_block
+    return jnp.where(mine, line, 0.0)
+
+
+def picks(table, ids, rounds, per_round):
+    own = one_hot(table, ids[0], rounds, per_round)
+    other = one_hot(table, ids[1], rounds, per_round)
+    weights = jnp.concatenate([own, other], axis=0)
+    return weights, jnp.where(weights != 0.0, 1.0, 0.0).astype(jnp.bfloat16)
+
+
+def select_kernel(count, rounds, per_round, ids_ref, *refs):
+    shards, (own_ref, other_ref) = refs[: 2 * count], refs[2 * count :]
+    for j in range(count):
+        token_ref, grad_ref = shards[2 * j], shards[2 * j + 1]
+        local, features = grad_ref.shape
+        table = token_ref[local:, :local]
+        weights, chosen = picks(table, ids_ref, rounds, per_round)
+        gate = jnp.sum(weights, axis=1, keepdims=True).astype(jnp.bfloat16)
+        gate = jnp.broadcast_to(gate, (2 * rounds, LANES))
+        left = dot(chosen, token_ref[:local, :], (1, 0)).astype(jnp.bfloat16)
+        right = dot(chosen, grad_ref[...], (1, 0)).astype(jnp.bfloat16)
+        for k, out in ((0, own_ref), (1, other_ref)):
+            lines = slice(j * rounds, (j + 1) * rounds)
+            half = slice(k * rounds, (k + 1) * rounds)
+            out[lines, :features] = left[half]
+            out[lines, features : 2 * features] = right[half]
+            out[lines, 2 * features :] = gate[half]
+
+
+def expert_kernel(ids_ref, own_ref, other_ref, w_in_ref, w_out_ref, grad_own, grad_other, x_ref, hid_ref, proj_ref, up_ref):
+    features, double = w_in_ref.shape
+    hidden_units = double // 2
+    rows = own_ref.shape[0]
+    w_in, w_out = w_in_ref[...], w_out_ref[...]
+    for start, ref, out in ((0, own_ref, grad_own), (rows, other_ref, grad_other)):
+        lines = slice(start, start + rows)
+        x = ref[:, :features]
+        upstream = ref[:, features : 2 * features]
+        gate = ref[:, 2 * features : 2 * features + 1].astype(jnp.float32)
+        projected = dot(x, w_in, (1, 0))
+        back_raw = dot(upstream, w_out, (1, 1))
+        gate_part, up_part = projected[:, :hidden_units], projected[:, hidden_units:]
+        activated, derivative = silu_parts(gate_part)
+        hidden = (activated * up_part).astype(jnp.bfloat16)
+        score = jnp.sum(hidden.astype(jnp.float32) * back_raw, axis=1, keepdims=True)
+        back_hidden = gate * back_raw
+        grad_projected = jnp.concatenate(
+            [back_hidden * up_part * derivative, back_hidden * activated], axis=1
+        ).astype(jnp.bfloat16)
+        x_ref[lines, :] = x
+        hid_ref[lines, :] = hidden
+        proj_ref[lines, :] = grad_projected
+        up_ref[lines, :] = (gate * upstream.astype(jnp.float32)).astype(jnp.bfloat16)
+        out[:, :features] = dot(grad_projected, w_in, (1, 1)).astype(jnp.bfloat16)
+        lane = lax.broadcasted_iota(jnp.int32, (rows, LANES), 1)
+        out[:, features:] = jnp.where(lane == ids_ref[0], score, 0.0).astype(jnp.bfloat16)
+
+
+def spread_kernel(count, rounds, per_round, ids_ref, own_ref, other_ref, *refs):
+    tables, outs = refs[:count], refs[count:]
+    for j in range(count):
+        local = outs[j].shape[0]
+        _, chosen = picks(tables[j][:, :local], ids_ref, rounds, per_round)
+        lines = slice(j * rounds, (j + 1) * rounds)
+        grads = jnp.concatenate([own_ref[lines, :], other_ref[lines, :]], axis=0)
+        outs[j][...] = dot(chosen, grads, (0, 0)).astype(jnp.bfloat16)
+
+
+def weights_kernel(groups, *refs):
+    ins, (grad_in_ref, grad_down_ref) = refs[: 4 * groups], refs[4 * groups :]
+    for out, left, right in ((grad_in_ref, 0, 2), (grad_down_ref, 1, 3)):
+        total = None
+        for g in range(groups):
+            part = dot(ins[4 * g + left][...], ins[4 * g + right][...], (0, 0))
+            total = part if total is None else total + part
+        out[0] = total.astype(jnp.bfloat16)
+
+
+def call(kernel, outs, args, smem=1, cost=None, specs=None):
+    in_specs = [pl.BlockSpec(memory_space=pltpu.SMEM)] * smem
+    in_specs += specs or [pl.BlockSpec(memory_space=pltpu.VMEM)] * (len(args) - smem)
+    return pl.pallas_call(
+        kernel,
+        out_shape=[jax.ShapeDtypeStruct(s, jnp.bfloat16) for s in outs],
+        grid=(1,) if specs else (),
+        in_specs=in_specs,
+        out_specs=[pl.BlockSpec(memory_space=pltpu.VMEM)] * len(outs),
+        compiler_params=pltpu.CompilerParams(vmem_limit_bytes=VMEM_LIMIT),
+        cost_estimate=cost,
+    )(*args)
+
+
+def ring_body(sizes, tokens, grad_out, routes, gates, w_gate_up, w_down):
+    first_size, second_size = sizes
+    columns = first_size // 2
+    local, features = tokens.shape
+    top_count = routes.shape[1]
+    experts = first_size * second_size
+    per_round = experts // top_count
+    rounds = local // per_round
+    hidden_units = w_gate_up.shape[2] // 2
+    ring = [(0, z) for z in range(second_size)] + [(1, z) for z in reversed(range(second_size))]
+    length = len(ring)
+
+    def device(place, core):
+        x, z = ring[place % length]
+        return (x * 2 + core) * second_size + z
+
+    def shift(value, step):
+        pairs = [(device(p, c), device(p + step, c)) for p in range(length) for c in range(2)]
+        return lax.ppermute(value, AXES, pairs)
+
+    def swap(value):
+        pairs = [(device(p, c), device(p, 1 - c)) for p in range(length) for c in range(2)]
+        return lax.ppermute(value, AXES, pairs)
+
+    me, row = lax.axis_index("da"), lax.axis_index("db")
+    core = lax.rem(me, 2)
+    ids = jnp.stack([me * second_size + row, (me + 1 - 2 * core) * second_size + row]).astype(jnp.int32)
+
+    expert_ids = lax.broadcasted_iota(jnp.int32, (experts, local, top_count), 0)
+    matches = routes[None] == expert_ids
+    table = jnp.sum(jnp.where(matches, gates[None].astype(jnp.float32), 0.0), axis=2).astype(jnp.bfloat16)
+    table = jnp.pad(table, ((0, 0), (0, features - local)))
+    first = jnp.concatenate([tokens, table], axis=0)
+
+    half = length // 2
+    shards = {0: (first, grad_out)}
+    right, left = (first, grad_out), (first, grad_out)
+    for step in range(1, half):
+        right = (shift(right[0], 1), shift(right[1], 1))
+        left = (shift(left[0], -1), shift(left[1], -1))
+        shards[-step], shards[step] = right, left
+    shards[half] = (shift(right[0], 1), shift(left[1], -1))
+
+    w_in, w_out = w_gate_up[0], w_down[0]
+    near = [0] + [s * k for k in range(1, half - 1) for s in (-1, 1)]
+    far = [1 - half, half - 1, half]
+    saved, sums = [], {}
+    wide = 2 * features + LANES
+    for group in (near, far):
+        count = len(group)
+        size = count * rounds
+        own, other = call(
+            functools.partial(select_kernel, count, rounds, per_round),
+            [(size, wide)] * 2,
+            [ids] + [a for k in group for a in shards[k]],
+        )
+        other = swap(other)
+        own_grad, other_grad, *kept = call(
+            expert_kernel,
+            [(size, features + LANES)] * 2
+            + [(2 * size, n) for n in (features, hidden_units, 2 * hidden_units, features)],
+            [ids, own, other, w_in, w_out],
+        )
+        saved += kept
+        other_grad = swap(other_grad)
+        table_spec = pl.BlockSpec((experts, LANES * pl.cdiv(local, LANES)), lambda i: (local // experts, 0))
+        spread = call(
+            functools.partial(spread_kernel, count, rounds, per_round),
+            [(local, features + LANES)] * count,
+            [ids, own_grad, other_grad] + [shards[k][0] for k in group],
+            specs=[pl.BlockSpec(memory_space=pltpu.VMEM)] * 2 + [table_spec] * count,
+        )
+        sums.update(zip(group, spread))
+
+    grad_in, grad_down = call(
+        functools.partial(weights_kernel, len(saved) // 4),
+        [(1, features, 2 * hidden_units), (1, hidden_units, features)],
+        saved,
+        smem=0,
+    )
+
+    def add(*terms):
+        return sum(t.astype(jnp.float32) for t in terms).astype(jnp.bfloat16)
+
+    cut = features // 2
+    right, left = shift(sums[half][:, :cut], 1), shift(sums[half][:, cut:], -1)
+    to_right, to_left = sums[half - 1], sums[1 - half]
+    right = jnp.concatenate([add(right, to_right[:, :cut]), to_right[:, cut:]], axis=1)
+    left = jnp.concatenate([to_left[:, :cut], add(left, to_left[:, cut:])], axis=1)
+    for k in range(half - 1, 0, -1):
+        right, left = shift(right, 1), shift(left, -1)
+        if k > 1:
+            right, left = add(right, sums[k - 1]), add(left, sums[1 - k])
+    total = add(right, left, sums[0])
+    scores = total[:, features : features + experts]
+    here = routes[:, :, None] == lax.broadcasted_iota(jnp.int32, (1, 1, experts), 2)
+    gate_grads = jnp.sum(jnp.where(here, scores[:, None, :].astype(jnp.float32), 0.0), axis=2).astype(jnp.bfloat16)
+    return total[:, :features], gate_grads, grad_in, grad_down
+
+
 def solution(mesh):
     placed = (
         P(("groups", "replica", "da", "db"), None),
@@ -107,8 +318,22 @@
         P(("da", "db"), "replica", None),
         P(("da", "db"), "replica", None),
     )
+    first_size, second_size = mesh.shape["da"], mesh.shape["db"]
+    experts = first_size * second_size
+
+    def chosen_body(tokens, grad_out, routes, gates, w_gate_up, w_down):
+        local, top_count = routes.shape
+        dense = experts // top_count <= 2
+        closed = mesh.shape["replica"] == 1 and first_size == 4 and second_size >= 2
+        fits = local % LANES == 0 and local <= tokens.shape[1] and experts % ROWS == 0 and local % experts == 0
+        fits = fits and experts <= LANES and (local * top_count // experts) % ROWS == 0
+        args = (tokens, grad_out, routes, gates, w_gate_up, w_down)
+        if dense and closed and fits:
+            return ring_body((first_size, second_size), *args)
+        return body(*args)
+
     return jax.shard_map(
-        body,
+        chosen_body,
         mesh=mesh,
         in_specs=placed,
         out_specs=(

time: 207 us -> 98.6 us (0.48)
  waiting for transfers between devices: 136 us -> 49.7 us
  local copies, waits for them, and re-layouts: 19.5 us -> 0.86 us
  matrix products: 18.6 us -> 0 us
  Pallas kernels: 0 us -> 17.3 us
  blocking collectives: 8.93 us -> 0 us
  starting transfers between devices: 20 us -> 26 us
    all_to_all x4 -> x0, waiting for transfers between devices: 136 us -> none  [the longest x1 46.1 us: body(): lax.all_to_all(input_send, ('da', 'db'), split_axis=1, concat_axis=1, til...]
    ppermute x0 -> x26, waiting for transfers between devices: none -> 49.7 us  [the longest x22 48 us: shift(): return lax.ppermute(value, AXES, pairs)]
    ppermute x0 -> x26, starting transfers between devices: none -> 26 us  [the longest x22 25.3 us: shift(): return lax.ppermute(value, AXES, pairs)]
    all_to_all x4 -> x0, starting transfers between devices: 20 us -> none  [the longest x1 7.54 us: body(): lax.all_to_all(input_send, ('da', 'db'), split_axis=1, concat_axis=1, til...]
    dot_general x8 -> x0, matrix products: 18.6 us -> none  [the longest x1 3.69 us: body(): jnp.einsum('rf,rd->fd', columns, scaled_upstream, preferred_element_type=...]
    pallas_call x0 -> x7, Pallas kernels: none -> 17.3 us  [call(): pl.pallas_call(kernel, out_shape=[jax.ShapeDtypeStruct(s, jnp.bfloat16) f...]
    all_to_all x1 -> x0, blocking collectives: 8.93 us -> none  [body(): lax.all_to_all(gate_table, ('da', 'db'), split_axis=1, concat_axis=1, til...]
    convert_element_type x10 -> x1, local copies, waits for them, and re-layouts: 6.2 us -> 0.05 us  [ring_body(): scores[:, None, :].astype(jnp.float32)]
  transfers between devices with their start and end apart: 4 -> 26, of which waited for: 4 -> 15; matrix products, arithmetic and copies ran while one was open for 8% -> 1% of each run, Pallas kernels for 0% -> 16%
where the time goes in v1:
time: 98.6 us; the launch traced here: 98.4 us
  waiting for transfers between devices  49.7 us (50%)
  starting transfers between devices  26 us (26%)
  Pallas kernels  17.3 us (18%)
  other arithmetic  3.64 us (4%)
    ppermute x22, waiting for transfers between devices, shift(): return lax.ppermute(value, AXES, pairs)  48 us
    ppermute x22, starting transfers between devices, shift(): return lax.ppermute(value, AXES, pairs)  25.3 us
    pallas_call x7, Pallas kernels, call(): pl.pallas_call(kernel, out_shape=[jax.ShapeDtypeStruct(s, jnp.bfloat16) f...  17.3 us
  transfers between devices with their start and end apart: 26, of which 15 were waited for; matrix products, arithmetic and copies ran while one was open for 1% of the time, Pallas kernels for 16%

profile of v1, /device:TPU:0, one launch (start us, length us, event | category | flops | bytes accessed | tf_op | source)
XLA Modules:
  0.0 98.4 jit_solution(7278124952074708851)
XLA Ops:
  3.1 3.1 %collective-permute-start = (bf16[144,1024]{1,0:T(8,128)(2,1)S(1)}, bf16[144,1024]{1,0:T(8,128)(2,1)S(1)}, u32[]{:S(2)}, u32[]{:S(2)}) collective-permute-start(bf16[144,1024]{1,0:T(8,128)(2,1)S(1)} %fusion.1.refs_0_), channel_id=1, source_target_pairs={{0,1},{4,5},{1,2},{5,6},{2,3},{6,7},{3,11},{7,15},{11,10},{15,14},... | collective-permute-start | bytes 884744 | tf_op jit(solution)/shard_map/ppermute | solution.py:230
  6.1 1.9 %collective-permute-start.6 = (bf16[144,1024]{1,0:T(8,128)(2,1)S(1)}, bf16[144,1024]{1,0:T(8,128)(2,1)S(1)}, u32[]{:S(2)}, u32[]{:S(2)}) collective-permute-start(bf16[144,1024]{1,0:T(8,128)(2,1)S(1)} %fusion.1.refs_0_), channel_id=1, source_target_pairs={{0,8},{4,12},{1,0},{5,4},{2,1},{6,5},{3,2},{7,6},{11,3},{15,7},{10... | collective-permute-start | bytes 884744 | tf_op jit(solution)/shard_map/ppermute | solution.py:230
  8.1 5.0 %collective-permute-done.refs_2_.refs_1_ = bf16[144,1024]{1,0:T(8,128)(2,1)S(1)} collective-permute-done((bf16[144,1024]{1,0:T(8,128)(2,1)S(1)}, bf16[144,1024]{1,0:T(8,128)(2,1)S(1)}, u32[]{:S(2)}, u32[]{:S(2)}) %collective-permute-start) | collective-permute-done | bytes 294944 | tf_op jit(solution)/shard_map/ppermute | solution.py:230
  13.1 1.8 %collective-permute-start.1 = (bf16[144,1024]{1,0:T(8,128)(2,1)S(1)}, bf16[144,1024]{1,0:T(8,128)(2,1)S(1)}, u32[]{:S(2)}, u32[]{:S(2)}) collective-permute-start(bf16[144,1024]{1,0:T(8,128)(2,1)S(1)} %collective-permute-done.refs_2_.refs_1_), channel_id=1, source_target_pairs={{0,1},{4,5},{1,2},{5,6},{2,3},{6,7},{3,11},{7,15},{11,10},{15,14},... | collective-permute-start | bytes 884744 | tf_op jit(solution)/shard_map/ppermute | solution.py:230
  16.9 5.0 %collective-permute-done.6.refs_4_.refs_2_ = bf16[144,1024]{1,0:T(8,128)(2,1)S(1)} collective-permute-done((bf16[144,1024]{1,0:T(8,128)(2,1)S(1)}, bf16[144,1024]{1,0:T(8,128)(2,1)S(1)}, u32[]{:S(2)}, u32[]{:S(2)}) %collective-permute-start.6) | collective-permute-done | bytes 294944 | tf_op jit(solution)/shard_map/ppermute | solution.py:230
  23.0 1.8 %collective-permute-start.2 = (bf16[144,1024]{1,0:T(8,128)(2,1)S(1)}, bf16[144,1024]{1,0:T(8,128)(2,1)S(1)}, u32[]{:S(2)}, u32[]{:S(2)}) collective-permute-start(bf16[144,1024]{1,0:T(8,128)(2,1)S(1)} %collective-permute-done.1.refs_6_.refs_3_), channel_id=1, source_target_pairs={{0,1},{4,5},{1,2},{5,6},{2,3},{6,7},{3,11},{7,15},{11,10},{15,14},... | collective-permute-start | bytes 884744 | tf_op jit(solution)/shard_map/ppermute | solution.py:230
  24.8 3.8 %collective-permute-done.3.refs_3_ = bf16[128,1024]{1,0:T(8,128)(2,1)S(1)} collective-permute-done((bf16[128,1024]{1,0:T(8,128)(2,1)}, bf16[128,1024]{1,0:T(8,128)(2,1)S(1)}, u32[]{:S(2)}, u32[]{:S(2)}) %collective-permute-start.3) | collective-permute-done | bytes 262176 | tf_op jit(solution)/shard_map/ppermute | solution.py:230
  28.6 1.8 %collective-permute-start.4 = (bf16[128,1024]{1,0:T(8,128)(2,1)S(1)}, bf16[128,1024]{1,0:T(8,128)(2,1)}, u32[]{:S(2)}, u32[]{:S(2)}) collective-permute-start(bf16[128,1024]{1,0:T(8,128)(2,1)S(1)} %collective-permute-done.3.refs_3_), channel_id=1, source_target_pairs={{0,1},{4,5},{1,2},{5,6},{2,3},{6,7},{3,11},{7,15},{11,10},{15,14},... | collective-permute-start | bytes 786440 | tf_op jit(solution)/shard_map/ppermute | solution.py:230
  30.7 3.2 %collective-permute-done.7.refs_8_.refs_4_ = bf16[144,1024]{1,0:T(8,128)(2,1)S(1)} collective-permute-done((bf16[144,1024]{1,0:T(8,128)(2,1)S(1)}, bf16[144,1024]{1,0:T(8,128)(2,1)S(1)}, u32[]{:S(2)}, u32[]{:S(2)}) %collective-permute-start.7) | collective-permute-done | bytes 294944 | tf_op jit(solution)/shard_map/ppermute | solution.py:230
  34.9 1.8 %collective-permute-start.12 = (bf16[144,1024]{1,0:T(8,128)(2,1)S(1)}, bf16[144,1024]{1,0:T(8,128)(2,1)S(1)}, u32[]{:S(2)}, u32[]{:S(2)}) collective-permute-start(bf16[144,1024]{1,0:T(8,128)(2,1)S(1)} %collective-permute-done.2.refs_0_), channel_id=1, source_target_pairs={{0,1},{4,5},{1,2},{5,6},{2,3},{6,7},{3,11},{7,15},{11,10},{15,14},... | collective-permute-start | bytes 884744 | tf_op jit(solution)/shard_map/ppermute | solution.py:230
  36.8 3.9 %collective-permute-done.4.refs_7_ = bf16[128,1024]{1,0:T(8,128)(2,1)} collective-permute-done((bf16[128,1024]{1,0:T(8,128)(2,1)S(1)}, bf16[128,1024]{1,0:T(8,128)(2,1)}, u32[]{:S(2)}, u32[]{:S(2)}) %collective-permute-start.4) | collective-permute-done | bytes 262176 | tf_op jit(solution)/shard_map/ppermute | solution.py:230
  40.7 1.8 %collective-permute-start.5 = (bf16[128,1024]{1,0:T(8,128)(2,1)}, bf16[128,1024]{1,0:T(8,128)(2,1)}, u32[]{:S(2)}, u32[]{:S(2)}) collective-permute-start(bf16[128,1024]{1,0:T(8,128)(2,1)} %collective-permute-done.4.refs_7_), channel_id=1, source_target_pairs={{0,1},{4,5},{1,2},{5,6},{2,3},{6,7},{3,11},{7,15},{11,10},{15,14},... | collective-permute-start | bytes 786440 | tf_op jit(solution)/shard_map/ppermute | solution.py:230
  42.8 8.1 %collective-permute-done.5.refs_1_ = bf16[128,1024]{1,0:T(8,128)(2,1)} collective-permute-done((bf16[128,1024]{1,0:T(8,128)(2,1)}, bf16[128,1024]{1,0:T(8,128)(2,1)}, u32[]{:S(2)}, u32[]{:S(2)}) %collective-permute-start.5) | collective-permute-done | bytes 262176 | tf_op jit(solution)/shard_map/ppermute | solution.py:230
  50.9 1.7 %shard_map.93 = (bf16[192,2176]{1,0:T(8,128)(2,1)S(1)}, bf16[192,2176]{1,0:T(8,128)(2,1)S(1)}) custom-call(s32[2]{0:T(128)S(1)} %pad_add_fusion.ids_ref, bf16[144,1024]{1,0:T(8,128)(2,1)S(1)} %collective-permute-done.2.refs_0_, bf16[128,1024]{1,0:T(8,128)(2,1)} %collective-permute-done.5.refs_1_, ...), custom_call_target="tpu_custom_call" | custom-call | tf_op jit(solution)/shard_map/pallas_call | solution.py:201
  52.7 1.9 %shard_map.96 = (bf16[320,2176]{1,0:T(8,128)(2,1)S(1)}, bf16[320,2176]{1,0:T(8,128)(2,1)S(1)}) custom-call(s32[2]{0:T(128)S(1)} %pad_add_fusion.ids_ref, bf16[144,1024]{1,0:T(8,128)(2,1)S(1)} %fusion.1.refs_0_, bf16[128,1024]{1,0:T(8,128)(2,1)S(1)} %copy-done.2, bf16[144,1024]{1,0:T(8,128)(2,1)S(1)} %collective-permute-done.refs_2_.refs_1_, ...), custom_call_target="tpu_custom_call" | custom-call | tf_op jit(solution)/shard_map/pallas_call | solution.py:201
  55.0 3.0 %shard_map.94 = (bf16[192,1152]{1,0:T(8,128)(2,1)S(1)}, bf16[192,1152]{1,0:T(8,128)(2,1)S(1)}, bf16[384,1024]{1,0:T(8,128)(2,1)S(1)}, bf16[384,384]{1,0:T(8,128)...) custom-call(s32[2]{0:T(128)S(1)} %pad_add_fusion.ids_ref, ...), custom_call_target="tpu_custom_call" | custom-call | tf_op jit(solution)/shard_map/pallas_call | solution.py:201
  58.2 1.6 %collective-permute-done.15.other_ref = bf16[192,1152]{1,0:T(8,128)(2,1)S(1)} collective-permute-done((bf16[192,1152]{1,0:T(8,128)(2,1)S(1)}, bf16[192,1152]{1,0:T(8,128)(2,1)S(1)}, u32[]{:S(2)}, u32[]{:S(2)}) %collective-permute-start.15) | collective-permute-done | bytes 442400 | tf_op jit(solution)/shard_map/ppermute | solution.py:234
  62.4 4.0 %shard_map.97 = (bf16[320,1152]{1,0:T(8,128)(2,1)S(1)}, bf16[320,1152]{1,0:T(8,128)(2,1)S(1)}, bf16[640,1024]{1,0:T(8,128)(2,1)S(1)}, bf16[640,384]{1,0:T(8,128)...) custom-call(s32[2]{0:T(128)S(1)} %pad_add_fusion.ids_ref, ...), custom_call_target="tpu_custom_call" | custom-call | tf_op jit(solution)/shard_map/pallas_call | solution.py:201
  68.7 4.4 %collective-permute-done.22 = bf16[128,640]{1,0:T(8,128)(2,1)S(1)} collective-permute-done((bf16[128,640]{1,0:T(8,128)(2,1)S(1)}, bf16[128,640]{1,0:T(8,128)(2,1)S(1)}, u32[]{:S(2)}, u32[]{:S(2)}) %collective-permute-start.22) | collective-permute-done | bytes 163872 | tf_op jit(solution)/shard_map/ppermute | solution.py:230
  78.0 3.9 %collective-permute-done.23 = bf16[128,1152]{1,0:T(8,128)(2,1)S(1)} collective-permute-done((bf16[128,1152]{1,0:T(8,128)(2,1)S(1)}, bf16[128,1152]{1,0:T(8,128)(2,1)S(1)}, u32[]{:S(2)}, u32[]{:S(2)}) %collective-permute-start.23) | collective-permute-done | bytes 294944 | tf_op jit(solution)/shard_map/ppermute | solution.py:230
  82.5 2.3 %collective-permute-done.20 = bf16[128,1152]{1,0:T(8,128)(2,1)S(1)} collective-permute-done((bf16[128,1152]{1,0:T(8,128)(2,1)S(1)}, bf16[128,1152]{1,0:T(8,128)(2,1)S(1)}, u32[]{:S(2)}, u32[]{:S(2)}) %collective-permute-start.20) | collective-permute-done | bytes 294944 | tf_op jit(solution)/shard_map/ppermute | solution.py:230
  86.4 3.3 %collective-permute-done.24 = bf16[128,1152]{1,0:T(8,128)(2,1)S(1)} collective-permute-done((bf16[128,1152]{1,0:T(8,128)(2,1)S(1)}, bf16[128,1152]{1,0:T(8,128)(2,1)S(1)}, u32[]{:S(2)}, u32[]{:S(2)}) %collective-permute-start.24) | collective-permute-done | bytes 294944 | tf_op jit(solution)/shard_map/ppermute | solution.py:230
  90.6 4.7 %shard_map.99 = (bf16[1,1024,768]{2,1,0:T(8,128)(2,1)}, bf16[1,384,1024]{2,1,0:T(8,128)(2,1)}) custom-call(bf16[640,1024]{1,0:T(8,128)(2,1)S(1)} %get-tuple-element.46.refs_0_, bf16[640,384]{1,0:T(8,128)(2,1)S(1)} %get-tuple-element.47.refs_1_, bf16[640,768]{1,0:T(8,128)(2,1)S(1)} %get-tuple-element.48.refs_2_, ...), custom_call_target="tpu_custom_call" | custom-call | tf_op jit(solution)/shard_map/pallas_call | solution.py:201
  95.3 1.6 %collective-permute-done.25 = bf16[128,1152]{1,0:T(8,128)(2,1)S(1)} collective-permute-done((bf16[128,1152]{1,0:T(8,128)(2,1)S(1)}, bf16[128,1152]{1,0:T(8,128)(2,1)S(1)}, u32[]{:S(2)}, u32[]{:S(2)}) %collective-permute-start.25) | collective-permute-done | bytes 294944 | tf_op jit(solution)/shard_map/ppermute | solution.py:230
  (64 shorter events, 22.2 us)
Async XLA Ops:
  3.1 10.0 %collective-permute-start = (bf16[144,1024]{1,0:T(8,128)(2,1)S(1)}, bf16[144,1024]{1,0:T(8,128)(2,1)S(1)}, u32[]{:S(2)}, u32[]{:S(2)}) collective-permute-start(bf16[144,1024]{1,0:T(8,128)(2,1)S(1)} %fusion.1.refs_0_), channel_id=1, source_target_pairs={{0,1},{4,5},{1,2},{5,6},{2,3},{6,7},{3,11},{7,15},{11,10},{15,14},... | collective-permute-start | bytes 884744 | tf_op jit(solution)/shard_map/ppermute | solution.py:230
  6.1 10.3 %collective-permute-start.9 = (bf16[128,1024]{1,0:T(8,128)(2,1)}, bf16[128,1024]{1,0:T(8,128)(2,1)S(1)}, u32[]{:S(2)}, u32[]{:S(2)}) collective-permute-start(bf16[128,1024]{1,0:T(8,128)(2,1)} %refs_1_.1), channel_id=1, source_target_pairs={{0,8},{4,12},{1,0},{5,4},{2,1},{6,5},{3,2},{7,6},{11,3},{15,7},{10... | collective-permute-start | bytes 786440 | tf_op jit(solution)/shard_map/ppermute | solution.py:230
  6.1 15.8 %collective-permute-start.6 = (bf16[144,1024]{1,0:T(8,128)(2,1)S(1)}, bf16[144,1024]{1,0:T(8,128)(2,1)S(1)}, u32[]{:S(2)}, u32[]{:S(2)}) collective-permute-start(bf16[144,1024]{1,0:T(8,128)(2,1)S(1)} %fusion.1.refs_0_), channel_id=1, source_target_pairs={{0,8},{4,12},{1,0},{5,4},{2,1},{6,5},{3,2},{7,6},{11,3},{15,7},{10... | collective-permute-start | bytes 884744 | tf_op jit(solution)/shard_map/ppermute | solution.py:230
  13.1 9.9 %collective-permute-start.1 = (bf16[144,1024]{1,0:T(8,128)(2,1)S(1)}, bf16[144,1024]{1,0:T(8,128)(2,1)S(1)}, u32[]{:S(2)}, u32[]{:S(2)}) collective-permute-start(bf16[144,1024]{1,0:T(8,128)(2,1)S(1)} %collective-permute-done.refs_2_.refs_1_), channel_id=1, source_target_pairs={{0,1},{4,5},{1,2},{5,6},{2,3},{6,7},{3,11},{7,15},{11,10},{15,14},... | collective-permute-start | bytes 884744 | tf_op jit(solution)/shard_map/ppermute | solution.py:230
  14.9 13.7 %collective-permute-start.3 = (bf16[128,1024]{1,0:T(8,128)(2,1)}, bf16[128,1024]{1,0:T(8,128)(2,1)S(1)}, u32[]{:S(2)}, u32[]{:S(2)}) collective-permute-start(bf16[128,1024]{1,0:T(8,128)(2,1)} %refs_1_.1), channel_id=1, source_target_pairs={{0,1},{4,5},{1,2},{5,6},{2,3},{6,7},{3,11},{7,15},{11,10},{15,14},... | collective-permute-start | bytes 786440 | tf_op jit(solution)/shard_map/ppermute | solution.py:230
  16.5 14.0 %collective-permute-start.10 = (bf16[128,1024]{1,0:T(8,128)(2,1)S(1)}, bf16[128,1024]{1,0:T(8,128)(2,1)S(1)}, u32[]{:S(2)}, u32[]{:S(2)}) collective-permute-start(bf16[128,1024]{1,0:T(8,128)(2,1)S(1)} %collective-permute-done.9.refs_5_), channel_id=1, source_target_pairs={{0,8},{4,12},{1,0},{5,4},{2,1},{6,5},{3,2},{7,6},{11,3},{15,7},{10... | collective-permute-start | bytes 786440 | tf_op jit(solution)/shard_map/ppermute | solution.py:230
  21.9 11.9 %collective-permute-start.7 = (bf16[144,1024]{1,0:T(8,128)(2,1)S(1)}, bf16[144,1024]{1,0:T(8,128)(2,1)S(1)}, u32[]{:S(2)}, u32[]{:S(2)}) collective-permute-start(bf16[144,1024]{1,0:T(8,128)(2,1)S(1)} %collective-permute-done.6.refs_4_.refs_2_), channel_id=1, source_target_pairs={{0,8},{4,12},{1,0},{5,4},{2,1},{6,5},{3,2},{7,6},{11,3},{15,7},{10... | collective-permute-start | bytes 884744 | tf_op jit(solution)/shard_map/ppermute | solution.py:230
  23.0 11.9 %collective-permute-start.2 = (bf16[144,1024]{1,0:T(8,128)(2,1)S(1)}, bf16[144,1024]{1,0:T(8,128)(2,1)S(1)}, u32[]{:S(2)}, u32[]{:S(2)}) collective-permute-start(bf16[144,1024]{1,0:T(8,128)(2,1)S(1)} %collective-permute-done.1.refs_6_.refs_3_), channel_id=1, source_target_pairs={{0,1},{4,5},{1,2},{5,6},{2,3},{6,7},{3,11},{7,15},{11,10},{15,14},... | collective-permute-start | bytes 884744 | tf_op jit(solution)/shard_map/ppermute | solution.py:230
  28.6 12.0 %collective-permute-start.4 = (bf16[128,1024]{1,0:T(8,128)(2,1)S(1)}, bf16[128,1024]{1,0:T(8,128)(2,1)}, u32[]{:S(2)}, u32[]{:S(2)}) collective-permute-start(bf16[128,1024]{1,0:T(8,128)(2,1)S(1)} %collective-permute-done.3.refs_3_), channel_id=1, source_target_pairs={{0,1},{4,5},{1,2},{5,6},{2,3},{6,7},{3,11},{7,15},{11,10},{15,14},... | collective-permute-start | bytes 786440 | tf_op jit(solution)/shard_map/ppermute | solution.py:230
  30.5 12.0 %collective-permute-start.11 = (bf16[128,1024]{1,0:T(8,128)(2,1)S(1)}, bf16[128,1024]{1,0:T(8,128)(2,1)}, u32[]{:S(2)}, u32[]{:S(2)}) collective-permute-start(bf16[128,1024]{1,0:T(8,128)(2,1)S(1)} %collective-permute-done.10.refs_9_), channel_id=1, source_target_pairs={{0,8},{4,12},{1,0},{5,4},{2,1},{6,5},{3,2},{7,6},{11,3},{15,7},{10... | collective-permute-start | bytes 786440 | tf_op jit(solution)/shard_map/ppermute | solution.py:230
  33.8 17.0 %collective-permute-start.8 = (bf16[144,1024]{1,0:T(8,128)(2,1)S(1)}, bf16[144,1024]{1,0:T(8,128)(2,1)S(1)}, u32[]{:S(2)}, u32[]{:S(2)}) collective-permute-start(bf16[144,1024]{1,0:T(8,128)(2,1)S(1)} %collective-permute-done.7.refs_8_.refs_4_), channel_id=1, source_target_pairs={{0,8},{4,12},{1,0},{5,4},{2,1},{6,5},{3,2},{7,6},{11,3},{15,7},{10... | collective-permute-start | bytes 884744 | tf_op jit(solution)/shard_map/ppermute | solution.py:230
  34.9 15.9 %collective-permute-start.12 = (bf16[144,1024]{1,0:T(8,128)(2,1)S(1)}, bf16[144,1024]{1,0:T(8,128)(2,1)S(1)}, u32[]{:S(2)}, u32[]{:S(2)}) collective-permute-start(bf16[144,1024]{1,0:T(8,128)(2,1)S(1)} %collective-permute-done.2.refs_0_), channel_id=1, source_target_pairs={{0,1},{4,5},{1,2},{5,6},{2,3},{6,7},{3,11},{7,15},{11,10},{15,14},... | collective-permute-start | bytes 884744 | tf_op jit(solution)/shard_map/ppermute | solution.py:230
  40.7 10.2 %collective-permute-start.5 = (bf16[128,1024]{1,0:T(8,128)(2,1)}, bf16[128,1024]{1,0:T(8,128)(2,1)}, u32[]{:S(2)}, u32[]{:S(2)}) collective-permute-start(bf16[128,1024]{1,0:T(8,128)(2,1)} %collective-permute-done.4.refs_7_), channel_id=1, source_target_pairs={{0,1},{4,5},{1,2},{5,6},{2,3},{6,7},{3,11},{7,15},{11,10},{15,14},... | collective-permute-start | bytes 786440 | tf_op jit(solution)/shard_map/ppermute | solution.py:230
  42.5 8.4 %collective-permute-start.13 = (bf16[128,1024]{1,0:T(8,128)(2,1)}, bf16[128,1024]{1,0:T(8,128)(2,1)}, u32[]{:S(2)}, u32[]{:S(2)}) collective-permute-start(bf16[128,1024]{1,0:T(8,128)(2,1)} %collective-permute-done.11.refs_3_), channel_id=1, source_target_pairs={{0,8},{4,12},{1,0},{5,4},{2,1},{6,5},{3,2},{7,6},{11,3},{15,7},{10... | collective-permute-start | bytes 786440 | tf_op jit(solution)/shard_map/ppermute | solution.py:230
  54.6 7.8 %collective-permute-start.18 = (bf16[320,2176]{1,0:T(8,128)(2,1)S(1)}, bf16[320,2176]{1,0:T(8,128)(2,1)S(1)}, u32[]{:S(2)}, u32[]{:S(2)}) collective-permute-start(bf16[320,2176]{1,0:T(8,128)(2,1)S(1)} %get-tuple-element.37), channel_id=1, source_target_pairs={{0,4},{4,0},{1,5},{5,1},{2,6},{6,2},{3,7},{7,3},{11,15},{15,11},{1... | collective-permute-start | bytes 4177928 | tf_op jit(solution)/shard_map/ppermute | solution.py:234
  60.9 6.2 %collective-permute-start.16 = (bf16[128,512]{1,0:T(8,128)(2,1)S(1)}, bf16[128,512]{1,0:T(8,128)(2,1)S(1)}, u32[]{:S(2)}, u32[]{:S(2)}) collective-permute-start(bf16[128,512]{1,0:T(8,128)(2,1)S(1)} %slice.24), channel_id=1, source_target_pairs={{0,1},{4,5},{1,2},{5,6},{2,3},{6,7},{3,11},{7,15},{11,10},{15,14},... | collective-permute-start | bytes 393224 | tf_op jit(solution)/shard_map/ppermute | solution.py:230
  66.4 7.4 %collective-permute-start.19 = (bf16[320,1152]{1,0:T(8,128)(2,1)S(1)}, bf16[320,1152]{1,0:T(8,128)(2,1)S(1)}, u32[]{:S(2)}, u32[]{:S(2)}) collective-permute-start(bf16[320,1152]{1,0:T(8,128)(2,1)S(1)} %get-tuple-element.39), channel_id=1, source_target_pairs={{0,4},{4,0},{1,5},{5,1},{2,6},{6,2},{3,7},{7,3},{11,15},{15,11},{1... | collective-permute-start | bytes 2211848 | tf_op jit(solution)/shard_map/ppermute | solution.py:234
  66.5 6.6 %collective-permute-start.22 = (bf16[128,640]{1,0:T(8,128)(2,1)S(1)}, bf16[128,640]{1,0:T(8,128)(2,1)S(1)}, u32[]{:S(2)}, u32[]{:S(2)}) collective-permute-start(bf16[128,640]{1,0:T(8,128)(2,1)S(1)} %slice.28), channel_id=1, source_target_pairs={{0,8},{4,12},{1,0},{5,4},{2,1},{6,5},{3,2},{7,6},{11,3},{15,7},{10... | collective-permute-start | bytes 491528 | tf_op jit(solution)/shard_map/ppermute | solution.py:230
  67.2 9.2 %collective-permute-start.17 = (bf16[128,1152]{1,0:T(8,128)(2,1)S(1)}, bf16[128,1152]{1,0:T(8,128)(2,1)S(1)}, u32[]{:S(2)}, u32[]{:S(2)}) collective-permute-start(bf16[128,1152]{1,0:T(8,128)(2,1)S(1)} %pad_maximum_fusion), channel_id=1, source_target_pairs={{0,1},{4,5},{1,2},{5,6},{2,3},{6,7},{3,11},{7,15},{11,10},{15,14},... | collective-permute-start | bytes 884744 | tf_op jit(solution)/shard_map/ppermute | solution.py:230
  73.2 8.7 %collective-permute-start.23 = (bf16[128,1152]{1,0:T(8,128)(2,1)S(1)}, bf16[128,1152]{1,0:T(8,128)(2,1)S(1)}, u32[]{:S(2)}, u32[]{:S(2)}) collective-permute-start(bf16[128,1152]{1,0:T(8,128)(2,1)S(1)} %pad_maximum_fusion.1), channel_id=1, source_target_pairs={{0,8},{4,12},{1,0},{5,4},{2,1},{6,5},{3,2},{7,6},{11,3},{15,7},{10... | collective-permute-start | bytes 884744 | tf_op jit(solution)/shard_map/ppermute | solution.py:230
  76.4 8.4 %collective-permute-start.20 = (bf16[128,1152]{1,0:T(8,128)(2,1)S(1)}, bf16[128,1152]{1,0:T(8,128)(2,1)S(1)}, u32[]{:S(2)}, u32[]{:S(2)}) collective-permute-start(bf16[128,1152]{1,0:T(8,128)(2,1)S(1)} %add_convert_fusion.4), channel_id=1, source_target_pairs={{0,1},{4,5},{1,2},{5,6},{2,3},{6,7},{3,11},{7,15},{11,10},{15,14},... | collective-permute-start | bytes 884744 | tf_op jit(solution)/shard_map/ppermute | solution.py:230
  82.0 7.8 %collective-permute-start.24 = (bf16[128,1152]{1,0:T(8,128)(2,1)S(1)}, bf16[128,1152]{1,0:T(8,128)(2,1)S(1)}, u32[]{:S(2)}, u32[]{:S(2)}) collective-permute-start(bf16[128,1152]{1,0:T(8,128)(2,1)S(1)} %add_convert_fusion.2), channel_id=1, source_target_pairs={{0,8},{4,12},{1,0},{5,4},{2,1},{6,5},{3,2},{7,6},{11,3},{15,7},{10... | collective-permute-start | bytes 884744 | tf_op jit(solution)/shard_map/ppermute | solution.py:230
  84.9 10.4 %collective-permute-start.21 = (bf16[128,1152]{1,0:T(8,128)(2,1)S(1)}, bf16[128,1152]{1,0:T(8,128)(2,1)S(1)}, u32[]{:S(2)}, u32[]{:S(2)}) collective-permute-start(bf16[128,1152]{1,0:T(8,128)(2,1)S(1)} %add_convert_fusion.3), channel_id=1, source_target_pairs={{0,1},{4,5},{1,2},{5,6},{2,3},{6,7},{3,11},{7,15},{11,10},{15,14},... | collective-permute-start | bytes 884744 | tf_op jit(solution)/shard_map/ppermute | solution.py:230
  89.8 7.0 %collective-permute-start.25 = (bf16[128,1152]{1,0:T(8,128)(2,1)S(1)}, bf16[128,1152]{1,0:T(8,128)(2,1)S(1)}, u32[]{:S(2)}, u32[]{:S(2)}) collective-permute-start(bf16[128,1152]{1,0:T(8,128)(2,1)S(1)} %add_convert_fusion.1), channel_id=1, source_target_pairs={{0,8},{4,12},{1,0},{5,4},{2,1},{6,5},{3,2},{7,6},{11,3},{15,7},{10... | collective-permute-start | bytes 884744 | tf_op jit(solution)/shard_map/ppermute | solution.py:230
  (6 other events, 63.7 us)

commit v2 on v0

--- a/solution.py
+++ b/solution.py
@@ -1,7 +1,18 @@
+import functools
+
 import jax
 import jax.numpy as jnp
 from jax import lax
+from jax.experimental import pallas as pl
+from jax.experimental.pallas import tpu as pltpu
 from jax.sharding import PartitionSpec as P
+
+LANES = 128
+ROWS = 16
+EXTRA = 8
+AXES = ("da", "db")
+VMEM_LIMIT = 40 * 1024 * 1024
+WHOLE_VMEM = 62 * 1024 * 1024
 
 
 def silu_parts(projected):
@@ -98,6 +109,300 @@
     return (token_grads, gate_grads, grad_in[None], grad_down[None])
 
 
+def dot(a, b, contract):
+    return lax.dot_general(a, b, ((contract[:1], contract[1:]), ((), ())), preferred_element_type=jnp.float32)
+
+
+def one_hot(table, expert, rounds, per_round):
+    experts, count = table.shape
+    rows = lax.broadcasted_iota(jnp.int32, (experts, count), 0)
+    line = jnp.sum(jnp.where(rows == expert, table, 0.0), axis=0, keepdims=True)
+    token_block = lax.broadcasted_iota(jnp.int32, (rounds, count), 1) // per_round
+    mine = lax.broadcasted_iota(jnp.int32, (rounds, count), 0) == token_block
+    return jnp.where(mine, line, 0.0)
+
+
+def fold(table, lanes):
+    experts, count = table.shape
+    parts = [table[k : k + EXTRA] for k in range(0, experts, EXTRA)]
+    used = count * len(parts)
+    if used < lanes:
+        parts.append(jnp.zeros((EXTRA, lanes - used), table.dtype))
+    return jnp.concatenate(parts, axis=1)
+
+
+def unfold(rows, experts, count):
+    return jnp.concatenate([rows[:, k * count : (k + 1) * count] for k in range(experts // EXTRA)], axis=0)
+
+
+def prepare_kernel(experts, token_hbm, grad_hbm, route_hbm, gate_hbm, out_ref, route_ref, gate_ref, sems):
+    local, features = token_hbm.shape
+    moves = (
+        (route_hbm, route_ref),
+        (gate_hbm, gate_ref),
+        (token_hbm, out_ref.at[pl.ds(0, local)]),
+        (grad_hbm, out_ref.at[pl.ds(local, local)]),
+    )
+    copies = [pltpu.make_async_copy(source, target, sems.at[k]) for k, (source, target) in enumerate(moves)]
+    for copy in copies:
+        copy.start()
+    for copy in copies[:2]:
+        copy.wait()
+    routes, gates = route_ref[...], gate_ref[...].astype(jnp.float32)
+    ids = lax.broadcasted_iota(jnp.int32, (experts, local), 0)
+    table = jnp.zeros((experts, local), jnp.float32)
+    for k in range(routes.shape[0]):
+        table += jnp.where(routes[k : k + 1] == ids, gates[k : k + 1], 0.0)
+    out_ref[2 * local :, :] = fold(table, features).astype(jnp.bfloat16)
+    for copy in copies[2:]:
+        copy.wait()
+
+
+def finish_kernel(experts, *refs):
+    route_ref, terms, (token_ref, gate_ref) = refs[0], refs[1:-2], refs[-2:]
+    local = token_ref.shape[0]
+    total = sum(term[...].astype(jnp.float32) for term in terms)
+    token_ref[...] = total[:local].astype(jnp.bfloat16)
+    scores = unfold(total[local:], experts, local)
+    routes = route_ref[...]
+    ids = lax.broadcasted_iota(jnp.int32, (experts, local), 0)
+    lines = [
+        jnp.sum(jnp.where(routes[k : k + 1] == ids, scores, 0.0), axis=0, keepdims=True)
+        for k in range(routes.shape[0])
+    ]
+    gate_ref[...] = jnp.concatenate(lines, axis=0).astype(jnp.bfloat16)
+
+
+def select_kernel(experts, rounds, per_round, ids_ref, *refs):
+    count = (len(refs) - 2) // 2
+    shards, (own_ref, other_ref), chosen_refs = refs[:count], refs[count : count + 2], refs[count + 2 :]
+    local = rounds * per_round
+    for j in range(count):
+        features = shards[j].shape[1]
+        table = unfold(shards[j][2 * local :, :].astype(jnp.float32), experts, local)
+        own = one_hot(table, ids_ref[0], rounds, per_round)
+        other = one_hot(table, ids_ref[1], rounds, per_round)
+        weights = jnp.concatenate([own, other], axis=0)
+        chosen = jnp.where(weights != 0.0, 1.0, 0.0).astype(jnp.bfloat16)
+        chosen_refs[j][...] = chosen
+        gate = jnp.sum(weights, axis=1, keepdims=True).astype(jnp.bfloat16)
+        gate = jnp.broadcast_to(gate, (2 * rounds, LANES))
+        for part in range(2):
+            picked = dot(chosen, shards[j][part * local : (part + 1) * local, :], (1, 0)).astype(jnp.bfloat16)
+            for k, out in ((0, own_ref), (1, other_ref)):
+                lines = slice(j * rounds, (j + 1) * rounds)
+                half = slice(k * rounds, (k + 1) * rounds)
+                out[lines, part * features : (part + 1) * features] = picked[half]
+                out[lines, 2 * features :] = gate[half]
+
+
+def expert_kernel(split, ids_ref, own_ref, other_ref, w_in_ref, w_out_ref, grad_own, grad_other, *kept_refs):
+    x_ref, hid_ref, proj_ref, up_ref = kept_refs
+    features, double = w_in_ref.shape
+    hidden_units = double // 2
+    size = own_ref.shape[0]
+    w_in, w_out = w_in_ref[...], w_out_ref[...]
+    both = ((own_ref, grad_own), (other_ref, grad_other))
+    start = 0
+    for part in [[pair] for pair in both] if split else [both]:
+        rows = size * len(part)
+        lines = slice(start, start + rows)
+        start += rows
+
+        def taken(begin, end):
+            return jnp.concatenate([ref[:, begin:end] for ref, _ in part], axis=0)
+
+        x, upstream = taken(0, features), taken(features, 2 * features)
+        gate = taken(2 * features, 2 * features + 1).astype(jnp.float32)
+        projected = dot(x, w_in, (1, 0))
+        back_raw = dot(upstream, w_out, (1, 1))
+        gate_part, up_part = projected[:, :hidden_units], projected[:, hidden_units:]
+        activated, derivative = silu_parts(gate_part)
+        hidden = (activated * up_part).astype(jnp.bfloat16)
+        score = jnp.sum(hidden.astype(jnp.float32) * back_raw, axis=1, keepdims=True)
+        back_hidden = gate * back_raw
+        grad_projected = jnp.concatenate(
+            [back_hidden * up_part * derivative, back_hidden * activated], axis=1
+        ).astype(jnp.bfloat16)
+        x_ref[lines, :] = x
+        hid_ref[lines, :] = hidden
+        proj_ref[lines, :] = grad_projected
+        up_ref[lines, :] = (gate * upstream.astype(jnp.float32)).astype(jnp.bfloat16)
+        input_grad = dot(grad_projected, w_in, (1, 1)).astype(jnp.bfloat16)
+        lane = lax.broadcasted_iota(jnp.int32, (rows, LANES), 1)
+        scores = jnp.where(lane == ids_ref[0], score, 0.0).astype(jnp.bfloat16)
+        for i, (_, out) in enumerate(part):
+            out[:, :features] = input_grad[i * size : (i + 1) * size]
+            out[:, features:] = scores[i * size : (i + 1) * size]
+
+
+def spread_kernel(experts, rounds, own_ref, other_ref, *refs):
+    count = len(refs) // 2
+    chosen_refs, outs = refs[:count], refs[count:]
+    for j in range(count):
+        lines = slice(j * rounds, (j + 1) * rounds)
+        chosen = chosen_refs[j][...]
+        local, features = chosen.shape[1], outs[j].shape[1]
+        grads = jnp.concatenate([own_ref[lines, :], other_ref[lines, :]], axis=0)
+        outs[j][:local, :] = dot(chosen, grads[:, :features], (0, 0)).astype(jnp.bfloat16)
+        scores = dot(grads[:, features:], chosen, (0, 0))[:experts]
+        outs[j][local:, :] = fold(scores, features).astype(jnp.bfloat16)
+
+
+def weights_kernel(begun, *refs):
+    sums, groups, outs = refs[: 2 * begun], refs[2 * begun : -2], refs[-2:]
+    for k, (left, right) in enumerate(((0, 2), (1, 3))):
+        total = sums[k][...] if begun else None
+        for g in range(0, len(groups), 4):
+            part = dot(groups[g + left][...], groups[g + right][...], (0, 0))
+            total = part if total is None else total + part
+        if begun:
+            outs[k][0] = total.astype(jnp.bfloat16)
+        else:
+            outs[k][...] = total
+
+
+def call(kernel, outs, args, smem=0, hbm=0, scratch=(), dtype=jnp.bfloat16, flops=0, vmem=VMEM_LIMIT):
+    in_specs = [pl.BlockSpec(memory_space=pltpu.SMEM)] * smem
+    in_specs += [pl.BlockSpec(memory_space=pltpu.HBM)] * hbm
+    in_specs += [pl.BlockSpec(memory_space=pltpu.VMEM)] * (len(args) - smem - hbm)
+    return pl.pallas_call(
+        kernel,
+        out_shape=[jax.ShapeDtypeStruct(s, dtype) for s in outs],
+        in_specs=in_specs,
+        out_specs=[pl.BlockSpec(memory_space=pltpu.VMEM)] * len(outs),
+        scratch_shapes=scratch,
+        compiler_params=pltpu.CompilerParams(vmem_limit_bytes=vmem),
+        cost_estimate=pl.CostEstimate(flops=flops, bytes_accessed=1 << 20, transcendentals=0),
+    )(*args)
+
+
+def ring_body(sizes, tokens, grad_out, routes, gates, w_gate_up, w_down):
+    first_size, second_size = sizes
+    local, features = tokens.shape
+    top_count = routes.shape[1]
+    experts = first_size * second_size
+    per_round = experts // top_count
+    rounds = local // per_round
+    hidden_units = w_gate_up.shape[2] // 2
+    ring = [(0, z) for z in range(second_size)] + [(1, z) for z in reversed(range(second_size))]
+    length = len(ring)
+    half = length // 2
+
+    def device(place, core):
+        x, z = ring[place % length]
+        return (x * 2 + core) * second_size + z
+
+    def shift(value, step):
+        pairs = [(device(p, c), device(p + (step if c == 0 else -step), c)) for p in range(length) for c in range(2)]
+        return lax.ppermute(value, AXES, pairs)
+
+    def swap(value):
+        pairs = [(device(p, c), device(p, 1 - c)) for p in range(length) for c in range(2)]
+        return lax.ppermute(value, AXES, pairs)
+
+    me, row = lax.axis_index("da"), lax.axis_index("db")
+    core = lax.rem(me, 2)
+    ids = jnp.stack([me * second_size + row, (me + 1 - 2 * core) * second_size + row]).astype(jnp.int32)
+
+    (message,) = call(
+        functools.partial(prepare_kernel, experts),
+        [(2 * local + EXTRA, features)],
+        [tokens, grad_out, routes.T, gates.T],
+        hbm=4,
+        vmem=WHOLE_VMEM,
+        scratch=[
+            pltpu.VMEM((top_count, local), routes.dtype),
+            pltpu.VMEM((top_count, local), gates.dtype),
+            pltpu.SemaphoreType.DMA((4,)),
+        ],
+    )
+    mine, theirs = {0: message}, {}
+    mine[1] = shift(mine[0], 1)
+    theirs[0] = swap(mine[0])
+    theirs[1] = shift(theirs[0], 1)
+    w_in, w_out = w_gate_up[0], w_down[0]
+    own_sums, other_sums = {}, {}
+
+    def work(group):
+        size = len(group) * rounds
+        shards = [(mine if own else theirs)[k] for own, k in group]
+        own, other, *chosen = call(
+            functools.partial(select_kernel, experts, rounds, per_round),
+            [(size, 2 * features + LANES)] * 2 + [(2 * rounds, local)] * len(group),
+            [ids] + shards,
+            smem=1,
+            flops=8 * 4 * size * local * 2 * features,
+        )
+        other = swap(other)
+        own_grad, other_grad, *kept = call(
+            functools.partial(expert_kernel, size > LANES),
+            [(size, features + LANES)] * 2
+            + [(2 * size, n) for n in (features, hidden_units, 2 * hidden_units, features)],
+            [ids, own, other, w_in, w_out],
+            smem=1,
+            flops=10 * 2 * 2 * size * features * 5 * hidden_units,
+        )
+        other_grad = swap(other_grad)
+        spread = call(
+            functools.partial(spread_kernel, experts, rounds),
+            [(local + EXTRA, features)] * len(group),
+            [own_grad, other_grad] + chosen,
+            flops=8 * 4 * size * local * features,
+        )
+        for (own, k), total in zip(group, spread):
+            (own_sums if own else other_sums)[k] = total
+        return kept
+
+    def after(value, *earlier):
+        return lax.optimization_barrier((value, *earlier))[0]
+
+    groups = [[(True, 0), (True, 1), (False, 1)]]
+    groups += [[(True, k), (False, k)] for k in range(2, half)] + [[(True, half)]]
+    kept, early = [], []
+    for k, group in enumerate(groups, 1):
+        if k < half:
+            mine[k + 1] = shift(mine[k], 1)
+            if k + 1 < half:
+                theirs[k + 1] = shift(theirs[k], 1)
+        if k == half - 1:
+            early = call(
+                functools.partial(weights_kernel, False),
+                [(features, 2 * hidden_units), (hidden_units, features)],
+                kept,
+                dtype=jnp.float32,
+                flops=10 * 2 * sum(x.shape[0] for x in kept[::4]) * features * 3 * hidden_units,
+            )
+            kept = []
+        if k == half:
+            mine[half] = after(mine[half], *early, *[v for k, v in own_sums.items() if k < half - 1], *[v for k, v in other_sums.items() if k < half - 1])
+        kept += work(group)
+
+    def add(*terms):
+        return sum(t.astype(jnp.float32) for t in terms).astype(jnp.bfloat16)
+
+    there, here = other_sums[half - 1], own_sums[half]
+    for k in range(half - 1, 0, -1):
+        there = shift(there, -1)
+        here = add(shift(here, -1), own_sums[k])
+        if k > 1:
+            there = add(there, other_sums[k - 1])
+    token_grads, gate_grads = call(
+        functools.partial(finish_kernel, experts),
+        [(local, features), (top_count, local)],
+        [routes.T, own_sums[0], swap(there), shift(here, -1)],
+    )
+
+    grad_in, grad_down = call(
+        functools.partial(weights_kernel, True),
+        [(1, features, 2 * hidden_units), (1, hidden_units, features)],
+        list(early) + kept,
+        smem=0,
+        flops=10 * 2 * sum(x.shape[0] for x in kept[::4]) * features * 3 * hidden_units,
+    )
+    return token_grads, gate_grads.T, grad_in, grad_down
+
+
 def solution(mesh):
     placed = (
         P(("groups", "replica", "da", "db"), None),
@@ -107,8 +412,22 @@
         P(("da", "db"), "replica", None),
         P(("da", "db"), "replica", None),
     )
+    first_size, second_size = mesh.shape["da"], mesh.shape["db"]
+    experts = first_size * second_size
+
+    def chosen_body(tokens, grad_out, routes, gates, w_gate_up, w_down):
+        local, top_count = routes.shape
+        dense = experts // top_count <= 2
+        closed = mesh.shape["replica"] == 1 and first_size == 4 and second_size >= 2
+        fits = local % LANES == 0 and experts % ROWS == 0 and experts <= LANES
+        fits = fits and experts * local <= EXTRA * tokens.shape[1] and (local * top_count // experts) % ROWS == 0
+        args = (tokens, grad_out, routes, gates, w_gate_up, w_down)
+        if dense and closed and fits:
+            return ring_body((first_size, second_size), *args)
+        return body(*args)
+
     return jax.shard_map(
-        body,
+        chosen_body,
         mesh=mesh,
         in_specs=placed,
         out_specs=(

time: 207 us -> 83 us (0.40)
  waiting for transfers between devices: 136 us -> 27 us
  Pallas kernels: 0 us -> 22 us
  matrix products: 18.6 us -> 0 us
  local copies, waits for them, and re-layouts: 19.5 us -> 1.06 us
  starting transfers between devices: 20 us -> 31.5 us
  blocking collectives: 8.93 us -> 0 us
  other arithmetic: 2.92 us -> 0.44 us
    all_to_all x4 -> x0, waiting for transfers between devices: 136 us -> none  [the longest x1 46.1 us: body(): lax.all_to_all(input_send, ('da', 'db'), split_axis=1, concat_axis=1, til...]
    ppermute x0 -> x24, starting transfers between devices: none -> 31.5 us  [the longest x14 29 us: shift(): return lax.ppermute(value, AXES, pairs)]
    ppermute x0 -> x24, waiting for transfers between devices: none -> 27 us  [the longest x14 26.9 us: shift(): return lax.ppermute(value, AXES, pairs)]
    pallas_call x0 -> x16, Pallas kernels: none -> 22 us  [call(): pl.pallas_call(kernel, out_shape=[jax.ShapeDtypeStruct(s, dtype) for s in...]
    all_to_all x4 -> x0, starting transfers between devices: 20 us -> none  [the longest x1 7.54 us: body(): lax.all_to_all(input_send, ('da', 'db'), split_axis=1, concat_axis=1, til...]
    dot_general x8 -> x0, matrix products: 18.6 us -> none  [the longest x1 3.69 us: body(): jnp.einsum('rf,rd->fd', columns, scaled_upstream, preferred_element_type=...]
    all_to_all x1 -> x0, blocking collectives: 8.93 us -> none  [body(): lax.all_to_all(gate_table, ('da', 'db'), split_axis=1, concat_axis=1, til...]
    convert_element_type x10 -> x0, local copies, waits for them, and re-layouts: 6.2 us -> none  [the longest x1 2.51 us: body(): upstream_send = jnp.einsum('rge,rgd->red', chosen, grad_out.reshape(round...]
  transfers between devices with their start and end apart: 4 -> 24, of which waited for: 4 -> 13; matrix products, arithmetic and copies ran while one was open for 8% -> 1% of each run, Pallas kernels for 0% -> 23%
where the time goes in v2:
time: 83 us; the launch traced here: 82.8 us
  starting transfers between devices  31.5 us (38%)
  waiting for transfers between devices  27 us (33%)
  Pallas kernels  22 us (27%)
  local copies, waits for them, and re-layouts  1.06 us (1%)
  between operations  0.86 us (1%)
    ppermute x14, starting transfers between devices, shift(): return lax.ppermute(value, AXES, pairs)  29 us
    ppermute x14, waiting for transfers between devices, shift(): return lax.ppermute(value, AXES, pairs)  26.9 us
    pallas_call x16, Pallas kernels, call(): pl.pallas_call(kernel, out_shape=[jax.ShapeDtypeStruct(s, dtype) for s in...  22 us
    ppermute x10, starting transfers between devices, swap(): return lax.ppermute(value, AXES, pairs)  2.54 us
  transfers between devices with their start and end apart: 24, of which 13 were waited for; matrix products, arithmetic and copies ran while one was open for 1% of the time, Pallas kernels for 23%

profile of v2, /device:TPU:0, one launch (start us, length us, event | category | flops | bytes accessed | tf_op | source)
XLA Modules:
  0.0 82.8 jit_solution(14397974151396331292)
XLA Ops:
  0.6 1.9 %shard_map.93.refs_0_ = bf16[264,1024]{1,0:T(8,128)(2,1)} custom-call(bf16[128,1024]{1,0:T(8,128)(2,1)} %token_hbm.1, bf16[128,1024]{1,0:T(8,128)(2,1)} %grad_hbm.1, s32[8,128]{1,0:T(8,128)} %bitcast.7, bf16[8,128]{1,0:T(8,128)(2,1)} %bitcast.17), custom_call_target="tpu_custom_call" | custom-call | bytes 1048576 | tf_op jit(solution)/shard_map/pallas_call | solution.py:269
  3.1 2.6 %collective-permute-start = (bf16[264,1024]{1,0:T(8,128)(2,1)}, bf16[264,1024]{1,0:T(8,128)(2,1)S(1)}, u32[]{:S(2)}, u32[]{:S(2)}) collective-permute-start(bf16[264,1024]{1,0:T(8,128)(2,1)} %shard_map.93.refs_0_), channel_id=1, source_target_pairs={{0,1},{4,12},{1,2},{5,4},{2,3},{6,5},{3,11},{7,6},{11,10},{15,7},{... | collective-permute-start | bytes 1622024 | tf_op jit(solution)/shard_map/ppermute | solution.py:298
  5.7 2.1 %collective-permute-start.2 = (bf16[264,1024]{1,0:T(8,128)(2,1)S(1)}, bf16[264,1024]{1,0:T(8,128)(2,1)S(1)}, u32[]{:S(2)}, u32[]{:S(2)}) collective-permute-start(bf16[264,1024]{1,0:T(8,128)(2,1)S(1)} %collective-permute-done.1), channel_id=1, source_target_pairs={{0,1},{4,12},{1,2},{5,4},{2,3},{6,5},{3,11},{7,6},{11,10},{15,7},{... | collective-permute-start | bytes 1622024 | tf_op jit(solution)/shard_map/ppermute | solution.py:298
  7.8 5.4 %collective-permute-done.refs_1_ = bf16[264,1024]{1,0:T(8,128)(2,1)S(1)} collective-permute-done((bf16[264,1024]{1,0:T(8,128)(2,1)}, bf16[264,1024]{1,0:T(8,128)(2,1)S(1)}, u32[]{:S(2)}, u32[]{:S(2)}) %collective-permute-start) | collective-permute-done | bytes 540704 | tf_op jit(solution)/shard_map/ppermute | solution.py:298
  13.1 2.1 %collective-permute-start.5 = (bf16[264,1024]{1,0:T(8,128)(2,1)S(1)}, bf16[264,1024]{1,0:T(8,128)(2,1)S(1)}, u32[]{:S(2)}, u32[]{:S(2)}) collective-permute-start(bf16[264,1024]{1,0:T(8,128)(2,1)S(1)} %collective-permute-done.refs_1_), channel_id=1, source_target_pairs={{0,1},{4,12},{1,2},{5,4},{2,3},{6,5},{3,11},{7,6},{11,10},{15,7},{... | collective-permute-start | bytes 1622024 | tf_op jit(solution)/shard_map/ppermute | solution.py:298
  15.3 3.6 %collective-permute-done.2.refs_2_ = bf16[264,1024]{1,0:T(8,128)(2,1)S(1)} collective-permute-done((bf16[264,1024]{1,0:T(8,128)(2,1)S(1)}, bf16[264,1024]{1,0:T(8,128)(2,1)S(1)}, u32[]{:S(2)}, u32[]{:S(2)}) %collective-permute-start.2) | collective-permute-done | bytes 540704 | tf_op jit(solution)/shard_map/ppermute | solution.py:298
  21.2 2.2 %collective-permute-start.7 = (bf16[264,1024]{1,0:T(8,128)(2,1)S(1)}, bf16[264,1024]{1,0:T(8,128)(2,1)S(1)}, u32[]{:S(2)}, u32[]{:S(2)}) collective-permute-start(bf16[264,1024]{1,0:T(8,128)(2,1)S(1)} %collective-permute-done.2.refs_2_), channel_id=1, source_target_pairs={{0,1},{4,12},{1,2},{5,4},{2,3},{6,5},{3,11},{7,6},{11,10},{15,7},{... | collective-permute-start | bytes 1622024 | tf_op jit(solution)/shard_map/ppermute | solution.py:298
  24.7 2.1 %collective-permute-start.6 = (bf16[264,1024]{1,0:T(8,128)(2,1)S(1)}, bf16[264,1024]{1,0:T(8,128)(2,1)S(1)}, u32[]{:S(2)}, u32[]{:S(2)}) collective-permute-start(bf16[264,1024]{1,0:T(8,128)(2,1)S(1)} %collective-permute-done.5.refs_0_), channel_id=1, source_target_pairs={{0,1},{4,12},{1,2},{5,4},{2,3},{6,5},{3,11},{7,6},{11,10},{15,7},{... | collective-permute-start | bytes 1622024 | tf_op jit(solution)/shard_map/ppermute | solution.py:298
  26.8 3.8 %collective-permute-done.7.refs_1_ = bf16[264,1024]{1,0:T(8,128)(2,1)S(1)} collective-permute-done((bf16[264,1024]{1,0:T(8,128)(2,1)S(1)}, bf16[264,1024]{1,0:T(8,128)(2,1)S(1)}, u32[]{:S(2)}, u32[]{:S(2)}) %collective-permute-start.7) | collective-permute-done | bytes 540704 | tf_op jit(solution)/shard_map/ppermute | solution.py:298
  31.6 2.2 %collective-permute-start.8 = (bf16[264,1024]{1,0:T(8,128)(2,1)S(1)}, bf16[264,1024]{1,0:T(8,128)(2,1)S(1)}, u32[]{:S(2)}, u32[]{:S(2)}) collective-permute-start(bf16[264,1024]{1,0:T(8,128)(2,1)S(1)} %collective-permute-done.7.refs_1_), channel_id=1, source_target_pairs={{0,1},{4,12},{1,2},{5,4},{2,3},{6,5},{3,11},{7,6},{11,10},{15,7},{... | collective-permute-start | bytes 1622024 | tf_op jit(solution)/shard_map/ppermute | solution.py:298
  33.8 2.6 %collective-permute-done.6.refs_0_ = bf16[264,1024]{1,0:T(8,128)(2,1)S(1)} collective-permute-done((bf16[264,1024]{1,0:T(8,128)(2,1)S(1)}, bf16[264,1024]{1,0:T(8,128)(2,1)S(1)}, u32[]{:S(2)}, u32[]{:S(2)}) %collective-permute-start.6) | collective-permute-done | bytes 540704 | tf_op jit(solution)/shard_map/ppermute | solution.py:298
  36.4 2.1 %collective-permute-start.17 = (bf16[264,1024]{1,0:T(8,128)(2,1)S(1)}, bf16[264,1024]{1,0:T(8,128)(2,1)S(1)}, u32[]{:S(2)}, u32[]{:S(2)}) collective-permute-start(bf16[264,1024]{1,0:T(8,128)(2,1)S(1)} %collective-permute-done.6.refs_0_), channel_id=1, source_target_pairs={{0,1},{4,12},{1,2},{5,4},{2,3},{6,5},{3,11},{7,6},{11,10},{15,7},{... | collective-permute-start | bytes 1622024 | tf_op jit(solution)/shard_map/ppermute | solution.py:298
  38.5 2.9 %shard_map.95 = (bf16[192,1152]{1,0:T(8,128)(2,1)S(1)}, bf16[192,1152]{1,0:T(8,128)(2,1)S(1)}, bf16[384,1024]{1,0:T(8,128)(2,1)S(1)}, bf16[384,384]{1,0:T(8,128)...) custom-call(s32[2]{0:T(128)S(1)} %pad_add_fusion.ids_ref, ...), custom_call_target="tpu_custom_call" | custom-call | flops 15099494400 | bytes 1048576 | tf_op jit(solution)/shard_map/pallas_call | solution.py:269
  41.5 2.3 %shard_map.101 = (bf16[128,1152]{1,0:T(8,128)(2,1)S(1)}, bf16[128,1152]{1,0:T(8,128)(2,1)S(1)}, bf16[256,1024]{1,0:T(8,128)(2,1)S(1)}, bf16[256,384]{1,0:T(8,128...) custom-call(s32[2]{0:T(128)S(1)} %pad_add_fusion.ids_ref, ...), custom_call_target="tpu_custom_call" | custom-call | flops 10066329600 | bytes 1048576 | tf_op jit(solution)/shard_map/pallas_call | solution.py:269
  44.4 2.0 %shard_map.103 = (f32[1024,768]{1,0:T(8,128)S(1)}, f32[384,1024]{1,0:T(8,128)S(1)}) custom-call(bf16[384,1024]{1,0:T(8,128)(2,1)S(1)} %get-tuple-element.81.refs_0_, bf16[384,384]{1,0:T(8,128)(2,1)S(1)} %get-tuple-element.82.refs_1_, bf16[384,768]{1,0:T(8,128)(2,1)S(1)} %get-tuple-element.83.refs_2_, bf16[384,1024]{1,0:T(8,128)(2,1)S(1)} %get-tuple-element.84.refs_3_, ...), custom_call_target="tpu_custom_call" | custom-call | flops 15099494400 | bytes 1048576 | tf_op jit(solution)/shard_map/pallas_call | solution.py:269
  52.3 2.3 %shard_map.98 = (bf16[128,1152]{1,0:T(8,128)(2,1)S(1)}, bf16[128,1152]{1,0:T(8,128)(2,1)S(1)}, bf16[256,1024]{1,0:T(8,128)(2,1)S(1)}, bf16[256,384]{1,0:T(8,128)...) custom-call(s32[2]{0:T(128)S(1)} %pad_add_fusion.ids_ref, ...), custom_call_target="tpu_custom_call" | custom-call | flops 10066329600 | bytes 1048576 | tf_op jit(solution)/shard_map/pallas_call | solution.py:269
  55.3 2.1 %collective-permute-start.20 = (bf16[136,1024]{1,0:T(8,128)(2,1)S(1)}, bf16[136,1024]{1,0:T(8,128)(2,1)S(1)}, u32[]{:S(2)}, u32[]{:S(2)}) collective-permute-start(bf16[136,1024]{1,0:T(8,128)(2,1)S(1)} %shard_map.106), channel_id=1, source_target_pairs={{0,8},{4,5},{1,0},{5,6},{2,1},{6,7},{3,2},{7,15},{11,3},{15,14},{1... | collective-permute-start | bytes 835592 | tf_op jit(solution)/shard_map/ppermute | solution.py:298
  59.4 2.6 %collective-permute-done.20 = bf16[136,1024]{1,0:T(8,128)(2,1)S(1)} collective-permute-done((bf16[136,1024]{1,0:T(8,128)(2,1)S(1)}, bf16[136,1024]{1,0:T(8,128)(2,1)S(1)}, u32[]{:S(2)}, u32[]{:S(2)}) %collective-permute-start.20) | collective-permute-done | bytes 278560 | tf_op jit(solution)/shard_map/ppermute | solution.py:298
  62.1 2.0 %collective-permute-start.21 = (bf16[136,1024]{1,0:T(8,128)(2,1)S(1)}, bf16[136,1024]{1,0:T(8,128)(2,1)S(1)}, u32[]{:S(2)}, u32[]{:S(2)}) collective-permute-start(bf16[136,1024]{1,0:T(8,128)(2,1)S(1)} %add_convert_fusion.2), channel_id=1, source_target_pairs={{0,8},{4,5},{1,0},{5,6},{2,1},{6,7},{3,2},{7,15},{11,3},{15,14},{1... | collective-permute-start | bytes 835592 | tf_op jit(solution)/shard_map/ppermute | solution.py:298
  65.1 2.0 %collective-permute-start.14 = (bf16[136,1024]{1,0:T(8,128)(2,1)S(1)}, bf16[136,1024]{1,0:T(8,128)(2,1)S(1)}, u32[]{:S(2)}, u32[]{:S(2)}) collective-permute-start(bf16[136,1024]{1,0:T(8,128)(2,1)S(1)} %add_convert_fusion.4), channel_id=1, source_target_pairs={{0,8},{4,5},{1,0},{5,6},{2,1},{6,7},{3,2},{7,15},{11,3},{15,14},{1... | collective-permute-start | bytes 835592 | tf_op jit(solution)/shard_map/ppermute | solution.py:298
  68.8 2.0 %collective-permute-start.22 = (bf16[136,1024]{1,0:T(8,128)(2,1)S(1)}, bf16[136,1024]{1,0:T(8,128)(2,1)S(1)}, u32[]{:S(2)}, u32[]{:S(2)}) collective-permute-start(bf16[136,1024]{1,0:T(8,128)(2,1)S(1)} %add_convert_fusion.1), channel_id=1, source_target_pairs={{0,8},{4,5},{1,0},{5,6},{2,1},{6,7},{3,2},{7,15},{11,3},{15,14},{1... | collective-permute-start | bytes 835592 | tf_op jit(solution)/shard_map/ppermute | solution.py:298
  71.7 2.0 %collective-permute-start.15 = (bf16[136,1024]{1,0:T(8,128)(2,1)S(1)}, bf16[136,1024]{1,0:T(8,128)(2,1)S(1)}, u32[]{:S(2)}, u32[]{:S(2)}) collective-permute-start(bf16[136,1024]{1,0:T(8,128)(2,1)S(1)} %add_convert_fusion.3), channel_id=1, source_target_pairs={{0,8},{4,5},{1,0},{5,6},{2,1},{6,7},{3,2},{7,15},{11,3},{15,14},{1... | collective-permute-start | bytes 835592 | tf_op jit(solution)/shard_map/ppermute | solution.py:298
  75.4 2.0 %collective-permute-start.23 = (bf16[136,1024]{1,0:T(8,128)(2,1)S(1)}, bf16[136,1024]{1,0:T(8,128)(2,1)S(1)}, u32[]{:S(2)}, u32[]{:S(2)}) collective-permute-start(bf16[136,1024]{1,0:T(8,128)(2,1)S(1)} %add_convert_fusion), channel_id=1, source_target_pairs={{0,8},{4,5},{1,0},{5,6},{2,1},{6,7},{3,2},{7,15},{11,3},{15,14},{1... | collective-permute-start | bytes 835592 | tf_op jit(solution)/shard_map/ppermute | solution.py:298
  78.3 2.9 %shard_map.108 = (bf16[1,1024,768]{2,1,0:T(8,128)(2,1)}, bf16[1,384,1024]{2,1,0:T(8,128)(2,1)}) custom-call(f32[1024,768]{1,0:T(8,128)S(1)} %get-tuple-element.89.refs_0_, f32[384,1024]{1,0:T(8,128)S(1)} %get-tuple-element.90.refs_1_, bf16[256,1024]{1,0:T(8,128)(2,1)S(1)} %get-tuple-element.102.refs_2_, bf16[256,384]{1,0:T(8,128)(2,1)S(1)} %get-tuple-element.103.refs_3_, ...), custom_call_target="tpu_custom_call" | custom-call | flops 9059696640 | bytes 1048576 | tf_op jit(solution)/shard_map/pallas_call | solution.py:269
  (54 shorter events, 22.4 us)
Async XLA Ops:
  2.5 3.2 %collective-permute-start.1 = (bf16[264,1024]{1,0:T(8,128)(2,1)}, bf16[264,1024]{1,0:T(8,128)(2,1)S(1)}, u32[]{:S(2)}, u32[]{:S(2)}) collective-permute-start(bf16[264,1024]{1,0:T(8,128)(2,1)} %shard_map.93.refs_0_), channel_id=1, source_target_pairs={{0,4},{4,0},{1,5},{5,1},{2,6},{6,2},{3,7},{7,3},{11,15},{15,11},{1... | collective-permute-start | bytes 1622024 | tf_op jit(solution)/shard_map/ppermute | solution.py:302
  3.1 10.1 %collective-permute-start = (bf16[264,1024]{1,0:T(8,128)(2,1)}, bf16[264,1024]{1,0:T(8,128)(2,1)S(1)}, u32[]{:S(2)}, u32[]{:S(2)}) collective-permute-start(bf16[264,1024]{1,0:T(8,128)(2,1)} %shard_map.93.refs_0_), channel_id=1, source_target_pairs={{0,1},{4,12},{1,2},{5,4},{2,3},{6,5},{3,11},{7,6},{11,10},{15,7},{... | collective-permute-start | bytes 1622024 | tf_op jit(solution)/shard_map/ppermute | solution.py:298
  5.7 13.3 %collective-permute-start.2 = (bf16[264,1024]{1,0:T(8,128)(2,1)S(1)}, bf16[264,1024]{1,0:T(8,128)(2,1)S(1)}, u32[]{:S(2)}, u32[]{:S(2)}) collective-permute-start(bf16[264,1024]{1,0:T(8,128)(2,1)S(1)} %collective-permute-done.1), channel_id=1, source_target_pairs={{0,1},{4,12},{1,2},{5,4},{2,3},{6,5},{3,11},{7,6},{11,10},{15,7},{... | collective-permute-start | bytes 1622024 | tf_op jit(solution)/shard_map/ppermute | solution.py:298
  13.1 11.6 %collective-permute-start.5 = (bf16[264,1024]{1,0:T(8,128)(2,1)S(1)}, bf16[264,1024]{1,0:T(8,128)(2,1)S(1)}, u32[]{:S(2)}, u32[]{:S(2)}) collective-permute-start(bf16[264,1024]{1,0:T(8,128)(2,1)S(1)} %collective-permute-done.refs_1_), channel_id=1, source_target_pairs={{0,1},{4,12},{1,2},{5,4},{2,3},{6,5},{3,11},{7,6},{11,10},{15,7},{... | collective-permute-start | bytes 1622024 | tf_op jit(solution)/shard_map/ppermute | solution.py:298
  21.1 17.4 %collective-permute-start.3 = (bf16[192,2176]{1,0:T(8,128)(2,1)S(1)}, bf16[192,2176]{1,0:T(8,128)(2,1)S(1)}, u32[]{:S(2)}, u32[]{:S(2)}) collective-permute-start(bf16[192,2176]{1,0:T(8,128)(2,1)S(1)} %get-tuple-element.59), channel_id=1, source_target_pairs={{0,4},{4,0},{1,5},{5,1},{2,6},{6,2},{3,7},{7,3},{11,15},{15,11},{1... | collective-permute-start | bytes 2506760 | tf_op jit(solution)/shard_map/ppermute | solution.py:302
  21.2 9.4 %collective-permute-start.7 = (bf16[264,1024]{1,0:T(8,128)(2,1)S(1)}, bf16[264,1024]{1,0:T(8,128)(2,1)S(1)}, u32[]{:S(2)}, u32[]{:S(2)}) collective-permute-start(bf16[264,1024]{1,0:T(8,128)(2,1)S(1)} %collective-permute-done.2.refs_2_), channel_id=1, source_target_pairs={{0,1},{4,12},{1,2},{5,4},{2,3},{6,5},{3,11},{7,6},{11,10},{15,7},{... | collective-permute-start | bytes 1622024 | tf_op jit(solution)/shard_map/ppermute | solution.py:298
  24.7 11.7 %collective-permute-start.6 = (bf16[264,1024]{1,0:T(8,128)(2,1)S(1)}, bf16[264,1024]{1,0:T(8,128)(2,1)S(1)}, u32[]{:S(2)}, u32[]{:S(2)}) collective-permute-start(bf16[264,1024]{1,0:T(8,128)(2,1)S(1)} %collective-permute-done.5.refs_0_), channel_id=1, source_target_pairs={{0,1},{4,12},{1,2},{5,4},{2,3},{6,5},{3,11},{7,6},{11,10},{15,7},{... | collective-permute-start | bytes 1622024 | tf_op jit(solution)/shard_map/ppermute | solution.py:298
  31.6 9.9 %collective-permute-start.12 = (bf16[128,2176]{1,0:T(8,128)(2,1)S(1)}, bf16[128,2176]{1,0:T(8,128)(2,1)S(1)}, u32[]{:S(2)}, u32[]{:S(2)}) collective-permute-start(bf16[128,2176]{1,0:T(8,128)(2,1)S(1)} %get-tuple-element.74), channel_id=1, source_target_pairs={{0,4},{4,0},{1,5},{5,1},{2,6},{6,2},{3,7},{7,3},{11,15},{15,11},{1... | collective-permute-start | bytes 1671176 | tf_op jit(solution)/shard_map/ppermute | solution.py:302
  31.6 17.2 %collective-permute-start.8 = (bf16[264,1024]{1,0:T(8,128)(2,1)S(1)}, bf16[264,1024]{1,0:T(8,128)(2,1)S(1)}, u32[]{:S(2)}, u32[]{:S(2)}) collective-permute-start(bf16[264,1024]{1,0:T(8,128)(2,1)S(1)} %collective-permute-done.7.refs_1_), channel_id=1, source_target_pairs={{0,1},{4,12},{1,2},{5,4},{2,3},{6,5},{3,11},{7,6},{11,10},{15,7},{... | collective-permute-start | bytes 1622024 | tf_op jit(solution)/shard_map/ppermute | solution.py:298
  36.4 11.6 %collective-permute-start.17 = (bf16[264,1024]{1,0:T(8,128)(2,1)S(1)}, bf16[264,1024]{1,0:T(8,128)(2,1)S(1)}, u32[]{:S(2)}, u32[]{:S(2)}) collective-permute-start(bf16[264,1024]{1,0:T(8,128)(2,1)S(1)} %collective-permute-done.6.refs_0_), channel_id=1, source_target_pairs={{0,1},{4,12},{1,2},{5,4},{2,3},{6,5},{3,11},{7,6},{11,10},{15,7},{... | collective-permute-start | bytes 1622024 | tf_op jit(solution)/shard_map/ppermute | solution.py:298
  41.4 5.0 %collective-permute-start.4 = (bf16[192,1152]{1,0:T(8,128)(2,1)S(1)}, bf16[192,1152]{1,0:T(8,128)(2,1)S(1)}, u32[]{:S(2)}, u32[]{:S(2)}) collective-permute-start(bf16[192,1152]{1,0:T(8,128)(2,1)S(1)} %get-tuple-element.61), channel_id=1, source_target_pairs={{0,4},{4,0},{1,5},{5,1},{2,6},{6,2},{3,7},{7,3},{11,15},{15,11},{1... | collective-permute-start | bytes 1327112 | tf_op jit(solution)/shard_map/ppermute | solution.py:302
  43.8 3.0 %collective-permute-start.13 = (bf16[128,1152]{1,0:T(8,128)(2,1)S(1)}, bf16[128,1152]{1,0:T(8,128)(2,1)S(1)}, u32[]{:S(2)}, u32[]{:S(2)}) collective-permute-start(bf16[128,1152]{1,0:T(8,128)(2,1)S(1)} %get-tuple-element.76), channel_id=1, source_target_pairs={{0,4},{4,0},{1,5},{5,1},{2,6},{6,2},{3,7},{7,3},{11,15},{15,11},{1... | collective-permute-start | bytes 884744 | tf_op jit(solution)/shard_map/ppermute | solution.py:302
  48.8 1.6 %collective-permute-start.18 = (bf16[64,2176]{1,0:T(8,128)(2,1)S(1)}, bf16[64,2176]{1,0:T(8,128)(2,1)S(1)}, u32[]{:S(2)}, u32[]{:S(2)}) collective-permute-start(bf16[64,2176]{1,0:T(8,128)(2,1)S(1)} %get-tuple-element.95), channel_id=1, source_target_pairs={{0,4},{4,0},{1,5},{5,1},{2,6},{6,2},{3,7},{7,3},{11,15},{15,11},{1... | collective-permute-start | bytes 835592 | tf_op jit(solution)/shard_map/ppermute | solution.py:302
  49.9 2.5 %collective-permute-start.9 = (bf16[128,2176]{1,0:T(8,128)(2,1)S(1)}, bf16[128,2176]{1,0:T(8,128)(2,1)S(1)}, u32[]{:S(2)}, u32[]{:S(2)}) collective-permute-start(bf16[128,2176]{1,0:T(8,128)(2,1)S(1)} %get-tuple-element.67), channel_id=1, source_target_pairs={{0,4},{4,0},{1,5},{5,1},{2,6},{6,2},{3,7},{7,3},{11,15},{15,11},{1... | collective-permute-start | bytes 1671176 | tf_op jit(solution)/shard_map/ppermute | solution.py:302
  52.1 2.9 %collective-permute-start.19 = (bf16[64,1152]{1,0:T(8,128)(2,1)S(1)}, bf16[64,1152]{1,0:T(8,128)(2,1)S(1)}, u32[]{:S(2)}, u32[]{:S(2)}) collective-permute-start(bf16[64,1152]{1,0:T(8,128)(2,1)S(1)} %get-tuple-element.97), channel_id=1, source_target_pairs={{0,4},{4,0},{1,5},{5,1},{2,6},{6,2},{3,7},{7,3},{11,15},{15,11},{1... | collective-permute-start | bytes 442376 | tf_op jit(solution)/shard_map/ppermute | solution.py:302
  54.6 2.8 %collective-permute-start.10 = (bf16[128,1152]{1,0:T(8,128)(2,1)S(1)}, bf16[128,1152]{1,0:T(8,128)(2,1)S(1)}, u32[]{:S(2)}, u32[]{:S(2)}) collective-permute-start(bf16[128,1152]{1,0:T(8,128)(2,1)S(1)} %get-tuple-element.69), channel_id=1, source_target_pairs={{0,4},{4,0},{1,5},{5,1},{2,6},{6,2},{3,7},{7,3},{11,15},{15,11},{1... | collective-permute-start | bytes 884744 | tf_op jit(solution)/shard_map/ppermute | solution.py:302
  55.3 6.7 %collective-permute-start.20 = (bf16[136,1024]{1,0:T(8,128)(2,1)S(1)}, bf16[136,1024]{1,0:T(8,128)(2,1)S(1)}, u32[]{:S(2)}, u32[]{:S(2)}) collective-permute-start(bf16[136,1024]{1,0:T(8,128)(2,1)S(1)} %shard_map.106), channel_id=1, source_target_pairs={{0,8},{4,5},{1,0},{5,6},{2,1},{6,7},{3,2},{7,15},{11,3},{15,14},{1... | collective-permute-start | bytes 835592 | tf_op jit(solution)/shard_map/ppermute | solution.py:298
  57.7 7.3 %collective-permute-start.11 = (bf16[136,1024]{1,0:T(8,128)(2,1)S(1)}, bf16[136,1024]{1,0:T(8,128)(2,1)S(1)}, u32[]{:S(2)}, u32[]{:S(2)}) collective-permute-start(bf16[136,1024]{1,0:T(8,128)(2,1)S(1)} %get-tuple-element.72), channel_id=1, source_target_pairs={{0,8},{4,5},{1,0},{5,6},{2,1},{6,7},{3,2},{7,15},{11,3},{15,14},{1... | collective-permute-start | bytes 835592 | tf_op jit(solution)/shard_map/ppermute | solution.py:298
  62.1 6.6 %collective-permute-start.21 = (bf16[136,1024]{1,0:T(8,128)(2,1)S(1)}, bf16[136,1024]{1,0:T(8,128)(2,1)S(1)}, u32[]{:S(2)}, u32[]{:S(2)}) collective-permute-start(bf16[136,1024]{1,0:T(8,128)(2,1)S(1)} %add_convert_fusion.2), channel_id=1, source_target_pairs={{0,8},{4,5},{1,0},{5,6},{2,1},{6,7},{3,2},{7,15},{11,3},{15,14},{1... | collective-permute-start | bytes 835592 | tf_op jit(solution)/shard_map/ppermute | solution.py:298
  65.1 6.6 %collective-permute-start.14 = (bf16[136,1024]{1,0:T(8,128)(2,1)S(1)}, bf16[136,1024]{1,0:T(8,128)(2,1)S(1)}, u32[]{:S(2)}, u32[]{:S(2)}) collective-permute-start(bf16[136,1024]{1,0:T(8,128)(2,1)S(1)} %add_convert_fusion.4), channel_id=1, source_target_pairs={{0,8},{4,5},{1,0},{5,6},{2,1},{6,7},{3,2},{7,15},{11,3},{15,14},{1... | collective-permute-start | bytes 835592 | tf_op jit(solution)/shard_map/ppermute | solution.py:298
  68.8 6.6 %collective-permute-start.22 = (bf16[136,1024]{1,0:T(8,128)(2,1)S(1)}, bf16[136,1024]{1,0:T(8,128)(2,1)S(1)}, u32[]{:S(2)}, u32[]{:S(2)}) collective-permute-start(bf16[136,1024]{1,0:T(8,128)(2,1)S(1)} %add_convert_fusion.1), channel_id=1, source_target_pairs={{0,8},{4,5},{1,0},{5,6},{2,1},{6,7},{3,2},{7,15},{11,3},{15,14},{1... | collective-permute-start | bytes 835592 | tf_op jit(solution)/shard_map/ppermute | solution.py:298
  71.7 6.6 %collective-permute-start.15 = (bf16[136,1024]{1,0:T(8,128)(2,1)S(1)}, bf16[136,1024]{1,0:T(8,128)(2,1)S(1)}, u32[]{:S(2)}, u32[]{:S(2)}) collective-permute-start(bf16[136,1024]{1,0:T(8,128)(2,1)S(1)} %add_convert_fusion.3), channel_id=1, source_target_pairs={{0,8},{4,5},{1,0},{5,6},{2,1},{6,7},{3,2},{7,15},{11,3},{15,14},{1... | collective-permute-start | bytes 835592 | tf_op jit(solution)/shard_map/ppermute | solution.py:298
  75.4 6.6 %collective-permute-start.23 = (bf16[136,1024]{1,0:T(8,128)(2,1)S(1)}, bf16[136,1024]{1,0:T(8,128)(2,1)S(1)}, u32[]{:S(2)}, u32[]{:S(2)}) collective-permute-start(bf16[136,1024]{1,0:T(8,128)(2,1)S(1)} %add_convert_fusion), channel_id=1, source_target_pairs={{0,8},{4,5},{1,0},{5,6},{2,1},{6,7},{3,2},{7,15},{11,3},{15,14},{1... | collective-permute-start | bytes 835592 | tf_op jit(solution)/shard_map/ppermute | solution.py:298
  78.3 3.7 %collective-permute-start.16 = (bf16[136,1024]{1,0:T(8,128)(2,1)S(1)}, bf16[136,1024]{1,0:T(8,128)(2,1)S(1)}, u32[]{:S(2)}, u32[]{:S(2)}) collective-permute-start(bf16[136,1024]{1,0:T(8,128)(2,1)S(1)} %collective-permute-done.15), channel_id=1, source_target_pairs={{0,4},{4,0},{1,5},{5,1},{2,6},{6,2},{3,7},{7,3},{11,15},{15,11},{1... | collective-permute-start | bytes 835592 | tf_op jit(solution)/shard_map/ppermute | solution.py:302
  (4 other events, 39.6 us)

commit v3 on v2

--- a/solution.py
+++ b/solution.py
@@ -196,12 +196,12 @@
                 out[lines, 2 * features :] = gate[half]
 
 
-def expert_kernel(split, ids_ref, own_ref, other_ref, w_in_ref, w_out_ref, grad_own, grad_other, *kept_refs):
+def expert_kernel(split, ids_ref, own_ref, other_ref, w_in_ref, back_in_ref, back_out_ref, grad_own, grad_other, *kept_refs):
     x_ref, hid_ref, proj_ref, up_ref = kept_refs
     features, double = w_in_ref.shape
     hidden_units = double // 2
     size = own_ref.shape[0]
-    w_in, w_out = w_in_ref[...], w_out_ref[...]
+    w_in, back_in, back_out = w_in_ref[...], back_in_ref[...], back_out_ref[...]
     both = ((own_ref, grad_own), (other_ref, grad_other))
     start = 0
     for part in [[pair] for pair in both] if split else [both]:
@@ -215,7 +215,7 @@
         x, upstream = taken(0, features), taken(features, 2 * features)
         gate = taken(2 * features, 2 * features + 1).astype(jnp.float32)
         projected = dot(x, w_in, (1, 0))
-        back_raw = dot(upstream, w_out, (1, 1))
+        back_raw = dot(upstream, back_out, (1, 0))
         gate_part, up_part = projected[:, :hidden_units], projected[:, hidden_units:]
         activated, derivative = silu_parts(gate_part)
         hidden = (activated * up_part).astype(jnp.bfloat16)
@@ -228,12 +228,17 @@
         hid_ref[lines, :] = hidden
         proj_ref[lines, :] = grad_projected
         up_ref[lines, :] = (gate * upstream.astype(jnp.float32)).astype(jnp.bfloat16)
-        input_grad = dot(grad_projected, w_in, (1, 1)).astype(jnp.bfloat16)
+        input_grad = dot(grad_projected, back_in, (1, 0)).astype(jnp.bfloat16)
         lane = lax.broadcasted_iota(jnp.int32, (rows, LANES), 1)
         scores = jnp.where(lane == ids_ref[0], score, 0.0).astype(jnp.bfloat16)
         for i, (_, out) in enumerate(part):
             out[:, :features] = input_grad[i * size : (i + 1) * size]
             out[:, features:] = scores[i * size : (i + 1) * size]
+
+
+def transpose_kernel(*refs):
+    for source, target in zip(refs[: len(refs) // 2], refs[len(refs) // 2 :]):
+        target[...] = source[...].T
 
 
 def spread_kernel(experts, rounds, own_ref, other_ref, *refs):
@@ -321,12 +326,20 @@
     mine[1] = shift(mine[0], 1)
     theirs[0] = swap(mine[0])
     theirs[1] = shift(theirs[0], 1)
+
+    def after(value, *earlier):
+        return lax.optimization_barrier((value, *earlier))[0]
+
     w_in, w_out = w_gate_up[0], w_down[0]
+    back_in, back_out = call(transpose_kernel, [w.shape[::-1] for w in (w_in, w_out)], [w_in, w_out])
+    mine[1] = after(mine[1], back_in, back_out)
     own_sums, other_sums = {}, {}
 
-    def work(group):
+    def pick(group, *earlier):
         size = len(group) * rounds
         shards = [(mine if own else theirs)[k] for own, k in group]
+        if earlier:
+            shards[-1] = after(shards[-1], *earlier)
         own, other, *chosen = call(
             functools.partial(select_kernel, experts, rounds, per_round),
             [(size, 2 * features + LANES)] * 2 + [(2 * rounds, local)] * len(group),
@@ -334,12 +347,15 @@
             smem=1,
             flops=8 * 4 * size * local * 2 * features,
         )
-        other = swap(other)
+        return group, size, own, swap(other), chosen
+
+    def work(picked):
+        group, size, own, other, chosen = picked
         own_grad, other_grad, *kept = call(
             functools.partial(expert_kernel, size > LANES),
             [(size, features + LANES)] * 2
             + [(2 * size, n) for n in (features, hidden_units, 2 * hidden_units, features)],
-            [ids, own, other, w_in, w_out],
+            [ids, own, other, w_in, back_in, back_out],
             smem=1,
             flops=10 * 2 * 2 * size * features * 5 * hidden_units,
         )
@@ -354,43 +370,38 @@
             (own_sums if own else other_sums)[k] = total
         return kept
 
-    def after(value, *earlier):
-        return lax.optimization_barrier((value, *earlier))[0]
-
-    groups = [[(True, 0), (True, 1), (False, 1)]]
-    groups += [[(True, k), (False, k)] for k in range(2, half)] + [[(True, half)]]
-    kept, early = [], []
-    for k, group in enumerate(groups, 1):
-        if k < half:
-            mine[k + 1] = shift(mine[k], 1)
-            if k + 1 < half:
-                theirs[k + 1] = shift(theirs[k], 1)
-        if k == half - 1:
-            early = call(
-                functools.partial(weights_kernel, False),
-                [(features, 2 * hidden_units), (hidden_units, features)],
-                kept,
-                dtype=jnp.float32,
-                flops=10 * 2 * sum(x.shape[0] for x in kept[::4]) * features * 3 * hidden_units,
-            )
-            kept = []
-        if k == half:
-            mine[half] = after(mine[half], *early, *[v for k, v in own_sums.items() if k < half - 1], *[v for k, v in other_sums.items() if k < half - 1])
-        kept += work(group)
+    for k in range(1, half):
+        mine[k + 1] = shift(mine[k], 1)
+        if k + 1 < half:
+            theirs[k + 1] = shift(theirs[k], 1)
+
+    near = [[(True, 0), (True, 1), (False, 1)]] + [[(True, k), (False, k)] for k in range(2, half - 1)]
+    kept = [array for group in near for array in work(pick(group))]
+    done = [*own_sums.values(), *other_sums.values()]
+    early = call(
+        functools.partial(weights_kernel, False),
+        [(features, 2 * hidden_units), (hidden_units, features)],
+        kept,
+        dtype=jnp.float32,
+        flops=10 * 2 * sum(x.shape[0] for x in kept[::4]) * features * 3 * hidden_units,
+    )
+    kept = work(pick([(True, half - 1), (False, half - 1)]))
+    kept = kept + work(pick([(True, half)], *done, kept[0]))
 
     def add(*terms):
         return sum(t.astype(jnp.float32) for t in terms).astype(jnp.bfloat16)
 
-    there, here = other_sums[half - 1], own_sums[half]
-    for k in range(half - 1, 0, -1):
-        there = shift(there, -1)
-        here = add(shift(here, -1), own_sums[k])
-        if k > 1:
-            there = add(there, other_sums[k - 1])
+    there, here = other_sums[half - 1], own_sums[half - 1]
+    far = shift(own_sums[half], -2)
+    for k in range(half - 2, -1, -1):
+        there, here = shift(there, -1), shift(here, -1)
+        if k > 0:
+            there = add(there, other_sums[k])
+            here = add(here, own_sums[k], far) if k == half - 2 else add(here, own_sums[k])
     token_grads, gate_grads = call(
         functools.partial(finish_kernel, experts),
         [(local, features), (top_count, local)],
-        [routes.T, own_sums[0], swap(there), shift(here, -1)],
+        [routes.T, own_sums[0], swap(there), here],
     )
 
     grad_in, grad_down = call(
@@ -418,7 +429,7 @@
     def chosen_body(tokens, grad_out, routes, gates, w_gate_up, w_down):
         local, top_count = routes.shape
         dense = experts // top_count <= 2
-        closed = mesh.shape["replica"] == 1 and first_size == 4 and second_size >= 2
+        closed = mesh.shape["replica"] == 1 and first_size == 4 and second_size >= 3
         fits = local % LANES == 0 and experts % ROWS == 0 and experts <= LANES
         fits = fits and experts * local <= EXTRA * tokens.shape[1] and (local * top_count // experts) % ROWS == 0
         args = (tokens, grad_out, routes, gates, w_gate_up, w_down)

time: 83 us -> 81.4 us (0.981)
  starting transfers between devices: 31.5 us -> 29.8 us
    ppermute x14, starting transfers between devices: 29 us -> 27.7 us  [shift(): return lax.ppermute(value, AXES, pairs)]
    pallas_call x16 -> x17, Pallas kernels: 22 us -> 21.3 us  [call(): pl.pallas_call(kernel, out_shape=[jax.ShapeDtypeStruct(s, dtype) for s in...]
  transfers between devices with their start and end apart: 24 -> 24, of which waited for: 13 -> 12; matrix products, arithmetic and copies ran while one was open for 1% -> 1% of each run, Pallas kernels for 23% -> 23%
where the time goes in v3:
time: 81.4 us; the launch traced here: 81.2 us
  starting transfers between devices  29.8 us (37%)
  waiting for transfers between devices  27.4 us (34%)
  Pallas kernels  21.3 us (26%)
  local copies, waits for them, and re-layouts  1.43 us (2%)
  between operations  0.86 us (1%)
    ppermute x14, starting transfers between devices, shift(): return lax.ppermute(value, AXES, pairs)  27.7 us
    ppermute x14, waiting for transfers between devices, shift(): return lax.ppermute(value, AXES, pairs)  27.4 us
    pallas_call x17, Pallas kernels, call(): pl.pallas_call(kernel, out_shape=[jax.ShapeDtypeStruct(s, dtype) for s in...  21.3 us
    ppermute x10, starting transfers between devices, swap(): return lax.ppermute(value, AXES, pairs)  2.06 us
  transfers between devices with their start and end apart: 24, of which 12 were waited for; matrix products, arithmetic and copies ran while one was open for 1% of the time, Pallas kernels for 23%

profile of v3, /device:TPU:0, one launch (start us, length us, event | category | flops | bytes accessed | tf_op | source)
XLA Modules:
  0.0 81.2 jit_solution(2914079227191977003)
XLA Ops:
  0.6 2.0 %shard_map.93.refs_0_ = bf16[264,1024]{1,0:T(8,128)(2,1)} custom-call(bf16[128,1024]{1,0:T(8,128)(2,1)} %token_hbm.1, bf16[128,1024]{1,0:T(8,128)(2,1)} %grad_hbm.1, s32[8,128]{1,0:T(8,128)} %bitcast.13, bf16[8,128]{1,0:T(8,128)(2,1)} %bitcast.15), custom_call_target="tpu_custom_call" | custom-call | bytes 1048576 | tf_op jit(solution)/shard_map/pallas_call | solution.py:274
  3.1 2.6 %collective-permute-start = (bf16[264,1024]{1,0:T(8,128)(2,1)}, bf16[264,1024]{1,0:T(8,128)(2,1)S(1)}, u32[]{:S(2)}, u32[]{:S(2)}) collective-permute-start(bf16[264,1024]{1,0:T(8,128)(2,1)} %shard_map.93.refs_0_), channel_id=1, source_target_pairs={{0,1},{4,12},{1,2},{5,4},{2,3},{6,5},{3,11},{7,6},{11,10},{15,7},{... | collective-permute-start | bytes 1622024 | tf_op jit(solution)/shard_map/ppermute | solution.py:303
  5.8 2.1 %collective-permute-start.2 = (bf16[264,1024]{1,0:T(8,128)(2,1)S(1)}, bf16[264,1024]{1,0:T(8,128)(2,1)S(1)}, u32[]{:S(2)}, u32[]{:S(2)}) collective-permute-start(bf16[264,1024]{1,0:T(8,128)(2,1)S(1)} %collective-permute-done.1), channel_id=1, source_target_pairs={{0,1},{4,12},{1,2},{5,4},{2,3},{6,5},{3,11},{7,6},{11,10},{15,7},{... | collective-permute-start | bytes 1622024 | tf_op jit(solution)/shard_map/ppermute | solution.py:303
  10.0 3.3 %collective-permute-done.refs_1_ = bf16[264,1024]{1,0:T(8,128)(2,1)S(1)} collective-permute-done((bf16[264,1024]{1,0:T(8,128)(2,1)}, bf16[264,1024]{1,0:T(8,128)(2,1)S(1)}, u32[]{:S(2)}, u32[]{:S(2)}) %collective-permute-start) | collective-permute-done | bytes 540704 | tf_op jit(solution)/shard_map/ppermute | solution.py:303
  13.2 2.1 %collective-permute-start.5 = (bf16[264,1024]{1,0:T(8,128)(2,1)S(1)}, bf16[264,1024]{1,0:T(8,128)(2,1)S(1)}, u32[]{:S(2)}, u32[]{:S(2)}) collective-permute-start(bf16[264,1024]{1,0:T(8,128)(2,1)S(1)} %collective-permute-done.refs_1_), channel_id=1, source_target_pairs={{0,1},{4,12},{1,2},{5,4},{2,3},{6,5},{3,11},{7,6},{11,10},{15,7},{... | collective-permute-start | bytes 1622024 | tf_op jit(solution)/shard_map/ppermute | solution.py:303
  15.4 3.6 %collective-permute-done.2.refs_2_ = bf16[264,1024]{1,0:T(8,128)(2,1)S(1)} collective-permute-done((bf16[264,1024]{1,0:T(8,128)(2,1)S(1)}, bf16[264,1024]{1,0:T(8,128)(2,1)S(1)}, u32[]{:S(2)}, u32[]{:S(2)}) %collective-permute-start.2) | collective-permute-done | bytes 540704 | tf_op jit(solution)/shard_map/ppermute | solution.py:303
  20.2 2.2 %collective-permute-start.7 = (bf16[264,1024]{1,0:T(8,128)(2,1)S(1)}, bf16[264,1024]{1,0:T(8,128)(2,1)S(1)}, u32[]{:S(2)}, u32[]{:S(2)}) collective-permute-start(bf16[264,1024]{1,0:T(8,128)(2,1)S(1)} %collective-permute-done.2.refs_2_), channel_id=1, source_target_pairs={{0,1},{4,12},{1,2},{5,4},{2,3},{6,5},{3,11},{7,6},{11,10},{15,7},{... | collective-permute-start | bytes 1622024 | tf_op jit(solution)/shard_map/ppermute | solution.py:303
  22.4 2.4 %collective-permute-done.5.refs_0_ = bf16[264,1024]{1,0:T(8,128)(2,1)S(1)} collective-permute-done((bf16[264,1024]{1,0:T(8,128)(2,1)S(1)}, bf16[264,1024]{1,0:T(8,128)(2,1)S(1)}, u32[]{:S(2)}, u32[]{:S(2)}) %collective-permute-start.5) | collective-permute-done | bytes 540704 | tf_op jit(solution)/shard_map/ppermute | solution.py:303
  24.8 2.1 %collective-permute-start.6 = (bf16[264,1024]{1,0:T(8,128)(2,1)S(1)}, bf16[264,1024]{1,0:T(8,128)(2,1)S(1)}, u32[]{:S(2)}, u32[]{:S(2)}) collective-permute-start(bf16[264,1024]{1,0:T(8,128)(2,1)S(1)} %collective-permute-done.5.refs_0_), channel_id=1, source_target_pairs={{0,1},{4,12},{1,2},{5,4},{2,3},{6,5},{3,11},{7,6},{11,10},{15,7},{... | collective-permute-start | bytes 1622024 | tf_op jit(solution)/shard_map/ppermute | solution.py:303
  26.9 3.7 %collective-permute-done.7.refs_1_ = bf16[264,1024]{1,0:T(8,128)(2,1)S(1)} collective-permute-done((bf16[264,1024]{1,0:T(8,128)(2,1)S(1)}, bf16[264,1024]{1,0:T(8,128)(2,1)S(1)}, u32[]{:S(2)}, u32[]{:S(2)}) %collective-permute-start.7) | collective-permute-done | bytes 540704 | tf_op jit(solution)/shard_map/ppermute | solution.py:303
  31.7 2.2 %collective-permute-start.8 = (bf16[264,1024]{1,0:T(8,128)(2,1)S(1)}, bf16[264,1024]{1,0:T(8,128)(2,1)S(1)}, u32[]{:S(2)}, u32[]{:S(2)}) collective-permute-start(bf16[264,1024]{1,0:T(8,128)(2,1)S(1)} %collective-permute-done.7.refs_1_), channel_id=1, source_target_pairs={{0,1},{4,12},{1,2},{5,4},{2,3},{6,5},{3,11},{7,6},{11,10},{15,7},{... | collective-permute-start | bytes 1622024 | tf_op jit(solution)/shard_map/ppermute | solution.py:303
  33.8 2.6 %collective-permute-done.6.refs_0_ = bf16[264,1024]{1,0:T(8,128)(2,1)S(1)} collective-permute-done((bf16[264,1024]{1,0:T(8,128)(2,1)S(1)}, bf16[264,1024]{1,0:T(8,128)(2,1)S(1)}, u32[]{:S(2)}, u32[]{:S(2)}) %collective-permute-start.6) | collective-permute-done | bytes 540704 | tf_op jit(solution)/shard_map/ppermute | solution.py:303
  36.4 2.1 %collective-permute-start.18 = (bf16[264,1024]{1,0:T(8,128)(2,1)S(1)}, bf16[264,1024]{1,0:T(8,128)(2,1)S(1)}, u32[]{:S(2)}, u32[]{:S(2)}) collective-permute-start(bf16[264,1024]{1,0:T(8,128)(2,1)S(1)} %collective-permute-done.6.refs_0_), channel_id=1, source_target_pairs={{0,1},{4,12},{1,2},{5,4},{2,3},{6,5},{3,11},{7,6},{11,10},{15,7},{... | collective-permute-start | bytes 1622024 | tf_op jit(solution)/shard_map/ppermute | solution.py:303
  38.5 2.6 %shard_map.96 = (bf16[192,1152]{1,0:T(8,128)(2,1)S(1)}, bf16[192,1152]{1,0:T(8,128)(2,1)S(1)}, bf16[384,1024]{1,0:T(8,128)(2,1)S(1)}, bf16[384,384]{1,0:T(8,128)...) custom-call(s32[2]{0:T(128)S(1)} %pad_add_fusion.ids_ref, ...), custom_call_target="tpu_custom_call" | custom-call | flops 15099494400 | bytes 1048576 | tf_op jit(solution)/shard_map/pallas_call | solution.py:274
  43.3 1.9 %shard_map.102 = (bf16[128,1152]{1,0:T(8,128)(2,1)S(1)}, bf16[128,1152]{1,0:T(8,128)(2,1)S(1)}, bf16[256,1024]{1,0:T(8,128)(2,1)S(1)}, bf16[256,384]{1,0:T(8,128...) custom-call(s32[2]{0:T(128)S(1)} %pad_add_fusion.ids_ref, ...), custom_call_target="tpu_custom_call" | custom-call | flops 10066329600 | bytes 1048576 | tf_op jit(solution)/shard_map/pallas_call | solution.py:274
  46.1 1.9 %shard_map.99 = (bf16[128,1152]{1,0:T(8,128)(2,1)S(1)}, bf16[128,1152]{1,0:T(8,128)(2,1)S(1)}, bf16[256,1024]{1,0:T(8,128)(2,1)S(1)}, bf16[256,384]{1,0:T(8,128)...) custom-call(s32[2]{0:T(128)S(1)} %pad_add_fusion.ids_ref, ...), custom_call_target="tpu_custom_call" | custom-call | flops 10066329600 | bytes 1048576 | tf_op jit(solution)/shard_map/pallas_call | solution.py:274
  50.2 2.1 %collective-permute-start.11 = (bf16[136,1024]{1,0:T(8,128)(2,1)S(1)}, bf16[136,1024]{1,0:T(8,128)(2,1)S(1)}, u32[]{:S(2)}, u32[]{:S(2)}) collective-permute-start(bf16[136,1024]{1,0:T(8,128)(2,1)S(1)} %get-tuple-element.78), channel_id=1, source_target_pairs={{0,8},{4,5},{1,0},{5,6},{2,1},{6,7},{3,2},{7,15},{11,3},{15,14},{1... | collective-permute-start | bytes 835592 | tf_op jit(solution)/shard_map/ppermute | solution.py:303
  53.8 1.6 %collective-permute-start.17 = (bf16[136,1024]{1,0:T(8,128)(2,1)S(1)}, bf16[136,1024]{1,0:T(8,128)(2,1)S(1)}, u32[]{:S(2)}, u32[]{:S(2)}) collective-permute-start(bf16[136,1024]{1,0:T(8,128)(2,1)S(1)} %get-tuple-element.87), channel_id=1, source_target_pairs={{0,8},{4,5},{1,0},{5,6},{2,1},{6,7},{3,2},{7,15},{11,3},{15,14},{1... | collective-permute-start | bytes 835592 | tf_op jit(solution)/shard_map/ppermute | solution.py:303
  55.7 2.6 %collective-permute-start.21 = (bf16[136,1024]{1,0:T(8,128)(2,1)S(1)}, bf16[136,1024]{1,0:T(8,128)(2,1)S(1)}, u32[]{:S(2)}, u32[]{:S(2)}) collective-permute-start(bf16[136,1024]{1,0:T(8,128)(2,1)S(1)} %shard_map.106), channel_id=1, source_target_pairs={{0,9},{4,6},{1,8},{5,7},{2,0},{6,15},{3,1},{7,14},{11,2},{15,13},{... | collective-permute-start | bytes 835592 | tf_op jit(solution)/shard_map/ppermute | solution.py:303
  60.4 5.1 %collective-permute-done.21 = bf16[136,1024]{1,0:T(8,128)(2,1)S(1)} collective-permute-done((bf16[136,1024]{1,0:T(8,128)(2,1)S(1)}, bf16[136,1024]{1,0:T(8,128)(2,1)S(1)}, u32[]{:S(2)}, u32[]{:S(2)}) %collective-permute-start.21) | collective-permute-done | bytes 278560 | tf_op jit(solution)/shard_map/ppermute | solution.py:303
  65.6 2.5 %collective-permute-start.22 = (bf16[136,1024]{1,0:T(8,128)(2,1)S(1)}, bf16[136,1024]{1,0:T(8,128)(2,1)S(1)}, u32[]{:S(2)}, u32[]{:S(2)}) collective-permute-start(bf16[136,1024]{1,0:T(8,128)(2,1)S(1)} %add_convert_fusion.1), channel_id=1, source_target_pairs={{0,8},{4,5},{1,0},{5,6},{2,1},{6,7},{3,2},{7,15},{11,3},{15,14},{1... | collective-permute-start | bytes 835592 | tf_op jit(solution)/shard_map/ppermute | solution.py:303
  70.4 2.0 %shard_map.108 = (f32[1024,768]{1,0:T(8,128)S(1)}, f32[384,1024]{1,0:T(8,128)S(1)}) custom-call(bf16[384,1024]{1,0:T(8,128)(2,1)S(1)} %get-tuple-element.99.refs_0_, bf16[384,384]{1,0:T(8,128)(2,1)S(1)} %get-tuple-element.100.refs_1_, bf16[384,768]{1,0:T(8,128)(2,1)S(1)} %get-tuple-element.101.refs_2_, bf16[384,1024]{1,0:T(8,128)(2,1)S(1)} %get-tuple-element.102.refs_3_, ...), custom_call_target="tpu_custom_call" | custom-call | flops 15099494400 | bytes 1048576 | tf_op jit(solution)/shard_map/pallas_call | solution.py:274
  75.1 1.7 %collective-permute-done.15 = bf16[136,1024]{1,0:T(8,128)(2,1)S(1)} collective-permute-done((bf16[136,1024]{1,0:T(8,128)(2,1)S(1)}, bf16[136,1024]{1,0:T(8,128)(2,1)S(1)}, u32[]{:S(2)}, u32[]{:S(2)}) %collective-permute-start.15) | collective-permute-done | bytes 278560 | tf_op jit(solution)/shard_map/ppermute | solution.py:303
  76.7 2.9 %shard_map.109 = (bf16[1,1024,768]{2,1,0:T(8,128)(2,1)}, bf16[1,384,1024]{2,1,0:T(8,128)(2,1)}) custom-call(f32[1024,768]{1,0:T(8,128)S(1)} %get-tuple-element.107.refs_0_, f32[384,1024]{1,0:T(8,128)S(1)} %get-tuple-element.108.refs_1_, bf16[256,1024]{1,0:T(8,128)(2,1)S(1)} %get-tuple-element.90.refs_2_, bf16[256,384]{1,0:T(8,128)(2,1)S(1)} %get-tuple-element.109.refs_3_, ...), custom_call_target="tpu_custom_call" | custom-call | flops 9059696640 | bytes 1048576 | tf_op jit(solution)/shard_map/pallas_call | solution.py:274
  (56 shorter events, 20.6 us)
Async XLA Ops:
  2.6 3.2 %collective-permute-start.1 = (bf16[264,1024]{1,0:T(8,128)(2,1)}, bf16[264,1024]{1,0:T(8,128)(2,1)S(1)}, u32[]{:S(2)}, u32[]{:S(2)}) collective-permute-start(bf16[264,1024]{1,0:T(8,128)(2,1)} %shard_map.93.refs_0_), channel_id=1, source_target_pairs={{0,4},{4,0},{1,5},{5,1},{2,6},{6,2},{3,7},{7,3},{11,15},{15,11},{1... | collective-permute-start | bytes 1622024 | tf_op jit(solution)/shard_map/ppermute | solution.py:307
  3.1 10.1 %collective-permute-start = (bf16[264,1024]{1,0:T(8,128)(2,1)}, bf16[264,1024]{1,0:T(8,128)(2,1)S(1)}, u32[]{:S(2)}, u32[]{:S(2)}) collective-permute-start(bf16[264,1024]{1,0:T(8,128)(2,1)} %shard_map.93.refs_0_), channel_id=1, source_target_pairs={{0,1},{4,12},{1,2},{5,4},{2,3},{6,5},{3,11},{7,6},{11,10},{15,7},{... | collective-permute-start | bytes 1622024 | tf_op jit(solution)/shard_map/ppermute | solution.py:303
  5.8 13.3 %collective-permute-start.2 = (bf16[264,1024]{1,0:T(8,128)(2,1)S(1)}, bf16[264,1024]{1,0:T(8,128)(2,1)S(1)}, u32[]{:S(2)}, u32[]{:S(2)}) collective-permute-start(bf16[264,1024]{1,0:T(8,128)(2,1)S(1)} %collective-permute-done.1), channel_id=1, source_target_pairs={{0,1},{4,12},{1,2},{5,4},{2,3},{6,5},{3,11},{7,6},{11,10},{15,7},{... | collective-permute-start | bytes 1622024 | tf_op jit(solution)/shard_map/ppermute | solution.py:303
  13.2 11.6 %collective-permute-start.5 = (bf16[264,1024]{1,0:T(8,128)(2,1)S(1)}, bf16[264,1024]{1,0:T(8,128)(2,1)S(1)}, u32[]{:S(2)}, u32[]{:S(2)}) collective-permute-start(bf16[264,1024]{1,0:T(8,128)(2,1)S(1)} %collective-permute-done.refs_1_), channel_id=1, source_target_pairs={{0,1},{4,12},{1,2},{5,4},{2,3},{6,5},{3,11},{7,6},{11,10},{15,7},{... | collective-permute-start | bytes 1622024 | tf_op jit(solution)/shard_map/ppermute | solution.py:303
  20.1 18.4 %collective-permute-start.3 = (bf16[192,2176]{1,0:T(8,128)(2,1)S(1)}, bf16[192,2176]{1,0:T(8,128)(2,1)S(1)}, u32[]{:S(2)}, u32[]{:S(2)}) collective-permute-start(bf16[192,2176]{1,0:T(8,128)(2,1)S(1)} %get-tuple-element.65), channel_id=1, source_target_pairs={{0,4},{4,0},{1,5},{5,1},{2,6},{6,2},{3,7},{7,3},{11,15},{15,11},{1... | collective-permute-start | bytes 2506760 | tf_op jit(solution)/shard_map/ppermute | solution.py:307
  20.2 10.4 %collective-permute-start.7 = (bf16[264,1024]{1,0:T(8,128)(2,1)S(1)}, bf16[264,1024]{1,0:T(8,128)(2,1)S(1)}, u32[]{:S(2)}, u32[]{:S(2)}) collective-permute-start(bf16[264,1024]{1,0:T(8,128)(2,1)S(1)} %collective-permute-done.2.refs_2_), channel_id=1, source_target_pairs={{0,1},{4,12},{1,2},{5,4},{2,3},{6,5},{3,11},{7,6},{11,10},{15,7},{... | collective-permute-start | bytes 1622024 | tf_op jit(solution)/shard_map/ppermute | solution.py:303
  24.8 11.6 %collective-permute-start.6 = (bf16[264,1024]{1,0:T(8,128)(2,1)S(1)}, bf16[264,1024]{1,0:T(8,128)(2,1)S(1)}, u32[]{:S(2)}, u32[]{:S(2)}) collective-permute-start(bf16[264,1024]{1,0:T(8,128)(2,1)S(1)} %collective-permute-done.5.refs_0_), channel_id=1, source_target_pairs={{0,1},{4,12},{1,2},{5,4},{2,3},{6,5},{3,11},{7,6},{11,10},{15,7},{... | collective-permute-start | bytes 1622024 | tf_op jit(solution)/shard_map/ppermute | solution.py:303
  31.6 11.7 %collective-permute-start.12 = (bf16[128,2176]{1,0:T(8,128)(2,1)S(1)}, bf16[128,2176]{1,0:T(8,128)(2,1)S(1)}, u32[]{:S(2)}, u32[]{:S(2)}) collective-permute-start(bf16[128,2176]{1,0:T(8,128)(2,1)S(1)} %get-tuple-element.80), channel_id=1, source_target_pairs={{0,4},{4,0},{1,5},{5,1},{2,6},{6,2},{3,7},{7,3},{11,15},{15,11},{1... | collective-permute-start | bytes 1671176 | tf_op jit(solution)/shard_map/ppermute | solution.py:307
  31.7 10.5 %collective-permute-start.8 = (bf16[264,1024]{1,0:T(8,128)(2,1)S(1)}, bf16[264,1024]{1,0:T(8,128)(2,1)S(1)}, u32[]{:S(2)}, u32[]{:S(2)}) collective-permute-start(bf16[264,1024]{1,0:T(8,128)(2,1)S(1)} %collective-permute-done.7.refs_1_), channel_id=1, source_target_pairs={{0,1},{4,12},{1,2},{5,4},{2,3},{6,5},{3,11},{7,6},{11,10},{15,7},{... | collective-permute-start | bytes 1622024 | tf_op jit(solution)/shard_map/ppermute | solution.py:303
  36.4 12.1 %collective-permute-start.18 = (bf16[264,1024]{1,0:T(8,128)(2,1)S(1)}, bf16[264,1024]{1,0:T(8,128)(2,1)S(1)}, u32[]{:S(2)}, u32[]{:S(2)}) collective-permute-start(bf16[264,1024]{1,0:T(8,128)(2,1)S(1)} %collective-permute-done.6.refs_0_), channel_id=1, source_target_pairs={{0,1},{4,12},{1,2},{5,4},{2,3},{6,5},{3,11},{7,6},{11,10},{15,7},{... | collective-permute-start | bytes 1622024 | tf_op jit(solution)/shard_map/ppermute | solution.py:303
  41.1 4.6 %collective-permute-start.4 = (bf16[192,1152]{1,0:T(8,128)(2,1)S(1)}, bf16[192,1152]{1,0:T(8,128)(2,1)S(1)}, u32[]{:S(2)}, u32[]{:S(2)}) collective-permute-start(bf16[192,1152]{1,0:T(8,128)(2,1)S(1)} %get-tuple-element.67), channel_id=1, source_target_pairs={{0,4},{4,0},{1,5},{5,1},{2,6},{6,2},{3,7},{7,3},{11,15},{15,11},{1... | collective-permute-start | bytes 1327112 | tf_op jit(solution)/shard_map/ppermute | solution.py:307
  43.2 3.0 %collective-permute-start.9 = (bf16[128,2176]{1,0:T(8,128)(2,1)S(1)}, bf16[128,2176]{1,0:T(8,128)(2,1)S(1)}, u32[]{:S(2)}, u32[]{:S(2)}) collective-permute-start(bf16[128,2176]{1,0:T(8,128)(2,1)S(1)} %get-tuple-element.73), channel_id=1, source_target_pairs={{0,4},{4,0},{1,5},{5,1},{2,6},{6,2},{3,7},{7,3},{11,15},{15,11},{1... | collective-permute-start | bytes 1671176 | tf_op jit(solution)/shard_map/ppermute | solution.py:307
  45.2 3.0 %collective-permute-start.13 = (bf16[128,1152]{1,0:T(8,128)(2,1)S(1)}, bf16[128,1152]{1,0:T(8,128)(2,1)S(1)}, u32[]{:S(2)}, u32[]{:S(2)}) collective-permute-start(bf16[128,1152]{1,0:T(8,128)(2,1)S(1)} %get-tuple-element.82), channel_id=1, source_target_pairs={{0,4},{4,0},{1,5},{5,1},{2,6},{6,2},{3,7},{7,3},{11,15},{15,11},{1... | collective-permute-start | bytes 884744 | tf_op jit(solution)/shard_map/ppermute | solution.py:307
  48.1 1.8 %collective-permute-start.10 = (bf16[128,1152]{1,0:T(8,128)(2,1)S(1)}, bf16[128,1152]{1,0:T(8,128)(2,1)S(1)}, u32[]{:S(2)}, u32[]{:S(2)}) collective-permute-start(bf16[128,1152]{1,0:T(8,128)(2,1)S(1)} %get-tuple-element.75), channel_id=1, source_target_pairs={{0,4},{4,0},{1,5},{5,1},{2,6},{6,2},{3,7},{7,3},{11,15},{15,11},{1... | collective-permute-start | bytes 884744 | tf_op jit(solution)/shard_map/ppermute | solution.py:307
  49.3 3.0 %collective-permute-start.19 = (bf16[64,2176]{1,0:T(8,128)(2,1)S(1)}, bf16[64,2176]{1,0:T(8,128)(2,1)S(1)}, u32[]{:S(2)}, u32[]{:S(2)}) collective-permute-start(bf16[64,2176]{1,0:T(8,128)(2,1)S(1)} %get-tuple-element.93), channel_id=1, source_target_pairs={{0,4},{4,0},{1,5},{5,1},{2,6},{6,2},{3,7},{7,3},{11,15},{15,11},{1... | collective-permute-start | bytes 835592 | tf_op jit(solution)/shard_map/ppermute | solution.py:307
  50.2 8.1 %collective-permute-start.11 = (bf16[136,1024]{1,0:T(8,128)(2,1)S(1)}, bf16[136,1024]{1,0:T(8,128)(2,1)S(1)}, u32[]{:S(2)}, u32[]{:S(2)}) collective-permute-start(bf16[136,1024]{1,0:T(8,128)(2,1)S(1)} %get-tuple-element.78), channel_id=1, source_target_pairs={{0,8},{4,5},{1,0},{5,6},{2,1},{6,7},{3,2},{7,15},{11,3},{15,14},{1... | collective-permute-start | bytes 835592 | tf_op jit(solution)/shard_map/ppermute | solution.py:303
  53.7 1.7 %collective-permute-start.20 = (bf16[64,1152]{1,0:T(8,128)(2,1)S(1)}, bf16[64,1152]{1,0:T(8,128)(2,1)S(1)}, u32[]{:S(2)}, u32[]{:S(2)}) collective-permute-start(bf16[64,1152]{1,0:T(8,128)(2,1)S(1)} %get-tuple-element.95), channel_id=1, source_target_pairs={{0,4},{4,0},{1,5},{5,1},{2,6},{6,2},{3,7},{7,3},{11,15},{15,11},{1... | collective-permute-start | bytes 442376 | tf_op jit(solution)/shard_map/ppermute | solution.py:307
  53.8 6.6 %collective-permute-start.17 = (bf16[136,1024]{1,0:T(8,128)(2,1)S(1)}, bf16[136,1024]{1,0:T(8,128)(2,1)S(1)}, u32[]{:S(2)}, u32[]{:S(2)}) collective-permute-start(bf16[136,1024]{1,0:T(8,128)(2,1)S(1)} %get-tuple-element.87), channel_id=1, source_target_pairs={{0,8},{4,5},{1,0},{5,6},{2,1},{6,7},{3,2},{7,15},{11,3},{15,14},{1... | collective-permute-start | bytes 835592 | tf_op jit(solution)/shard_map/ppermute | solution.py:303
  55.7 9.8 %collective-permute-start.21 = (bf16[136,1024]{1,0:T(8,128)(2,1)S(1)}, bf16[136,1024]{1,0:T(8,128)(2,1)S(1)}, u32[]{:S(2)}, u32[]{:S(2)}) collective-permute-start(bf16[136,1024]{1,0:T(8,128)(2,1)S(1)} %shard_map.106), channel_id=1, source_target_pairs={{0,9},{4,6},{1,8},{5,7},{2,0},{6,15},{3,1},{7,14},{11,2},{15,13},{... | collective-permute-start | bytes 835592 | tf_op jit(solution)/shard_map/ppermute | solution.py:303
  58.4 11.0 %collective-permute-start.14 = (bf16[136,1024]{1,0:T(8,128)(2,1)S(1)}, bf16[136,1024]{1,0:T(8,128)(2,1)S(1)}, u32[]{:S(2)}, u32[]{:S(2)}) collective-permute-start(bf16[136,1024]{1,0:T(8,128)(2,1)S(1)} %add_convert_fusion.3), channel_id=1, source_target_pairs={{0,8},{4,5},{1,0},{5,6},{2,1},{6,7},{3,2},{7,15},{11,3},{15,14},{1... | collective-permute-start | bytes 835592 | tf_op jit(solution)/shard_map/ppermute | solution.py:303
  65.6 8.1 %collective-permute-start.22 = (bf16[136,1024]{1,0:T(8,128)(2,1)S(1)}, bf16[136,1024]{1,0:T(8,128)(2,1)S(1)}, u32[]{:S(2)}, u32[]{:S(2)}) collective-permute-start(bf16[136,1024]{1,0:T(8,128)(2,1)S(1)} %add_convert_fusion.1), channel_id=1, source_target_pairs={{0,8},{4,5},{1,0},{5,6},{2,1},{6,7},{3,2},{7,15},{11,3},{15,14},{1... | collective-permute-start | bytes 835592 | tf_op jit(solution)/shard_map/ppermute | solution.py:303
  69.5 7.2 %collective-permute-start.15 = (bf16[136,1024]{1,0:T(8,128)(2,1)S(1)}, bf16[136,1024]{1,0:T(8,128)(2,1)S(1)}, u32[]{:S(2)}, u32[]{:S(2)}) collective-permute-start(bf16[136,1024]{1,0:T(8,128)(2,1)S(1)} %add_convert_fusion.2), channel_id=1, source_target_pairs={{0,8},{4,5},{1,0},{5,6},{2,1},{6,7},{3,2},{7,15},{11,3},{15,14},{1... | collective-permute-start | bytes 835592 | tf_op jit(solution)/shard_map/ppermute | solution.py:303
  73.8 6.6 %collective-permute-start.23 = (bf16[136,1024]{1,0:T(8,128)(2,1)S(1)}, bf16[136,1024]{1,0:T(8,128)(2,1)S(1)}, u32[]{:S(2)}, u32[]{:S(2)}) collective-permute-start(bf16[136,1024]{1,0:T(8,128)(2,1)S(1)} %add_convert_fusion), channel_id=1, source_target_pairs={{0,8},{4,5},{1,0},{5,6},{2,1},{6,7},{3,2},{7,15},{11,3},{15,14},{1... | collective-permute-start | bytes 835592 | tf_op jit(solution)/shard_map/ppermute | solution.py:303
  76.7 3.7 %collective-permute-start.16 = (bf16[136,1024]{1,0:T(8,128)(2,1)S(1)}, bf16[136,1024]{1,0:T(8,128)(2,1)S(1)}, u32[]{:S(2)}, u32[]{:S(2)}) collective-permute-start(bf16[136,1024]{1,0:T(8,128)(2,1)S(1)} %collective-permute-done.15), channel_id=1, source_target_pairs={{0,4},{4,0},{1,5},{5,1},{2,6},{6,2},{3,7},{7,3},{11,15},{15,11},{1... | collective-permute-start | bytes 835592 | tf_op jit(solution)/shard_map/ppermute | solution.py:307
  (5 other events, 40.5 us)

commit v4 on v3

--- a/solution.py
+++ b/solution.py
@@ -11,7 +11,7 @@
 ROWS = 16
 EXTRA = 8
 AXES = ("da", "db")
-VMEM_LIMIT = 40 * 1024 * 1024
+VMEM_LIMIT = 24 * 1024 * 1024
 WHOLE_VMEM = 62 * 1024 * 1024
 
 

time: 81.4 us -> 81.4 us (level)
  no operation moved by 1% of the time
where the time goes in v4:
time: 81.4 us; the launch traced here: 81.2 us
  starting transfers between devices  29.8 us (37%)
  waiting for transfers between devices  27.4 us (34%)
  Pallas kernels  21.3 us (26%)
  local copies, waits for them, and re-layouts  1.43 us (2%)
  between operations  0.86 us (1%)
    ppermute x14, starting transfers between devices, shift(): return lax.ppermute(value, AXES, pairs)  27.7 us
    ppermute x14, waiting for transfers between devices, shift(): return lax.ppermute(value, AXES, pairs)  27.4 us
    pallas_call x17, Pallas kernels, call(): pl.pallas_call(kernel, out_shape=[jax.ShapeDtypeStruct(s, dtype) for s in...  21.3 us
    ppermute x10, starting transfers between devices, swap(): return lax.ppermute(value, AXES, pairs)  2.06 us
  transfers between devices with their start and end apart: 24, of which 12 were waited for; matrix products, arithmetic and copies ran while one was open for 1% of the time, Pallas kernels for 23%

profile of v4, /device:TPU:0, one launch (start us, length us, event | category | flops | bytes accessed | tf_op | source)
XLA Modules:
  0.0 81.2 jit_solution(15377776814663358615)
XLA Ops:
  0.6 2.0 %shard_map.93.refs_0_ = bf16[264,1024]{1,0:T(8,128)(2,1)} custom-call(bf16[128,1024]{1,0:T(8,128)(2,1)} %token_hbm.1, bf16[128,1024]{1,0:T(8,128)(2,1)} %grad_hbm.1, s32[8,128]{1,0:T(8,128)} %bitcast.13, bf16[8,128]{1,0:T(8,128)(2,1)} %bitcast.15), custom_call_target="tpu_custom_call" | custom-call | bytes 1048576 | tf_op jit(solution)/shard_map/pallas_call | solution.py:274
  3.1 2.6 %collective-permute-start = (bf16[264,1024]{1,0:T(8,128)(2,1)}, bf16[264,1024]{1,0:T(8,128)(2,1)S(1)}, u32[]{:S(2)}, u32[]{:S(2)}) collective-permute-start(bf16[264,1024]{1,0:T(8,128)(2,1)} %shard_map.93.refs_0_), channel_id=1, source_target_pairs={{0,1},{4,12},{1,2},{5,4},{2,3},{6,5},{3,11},{7,6},{11,10},{15,7},{... | collective-permute-start | bytes 1622024 | tf_op jit(solution)/shard_map/ppermute | solution.py:303
  5.8 2.1 %collective-permute-start.2 = (bf16[264,1024]{1,0:T(8,128)(2,1)S(1)}, bf16[264,1024]{1,0:T(8,128)(2,1)S(1)}, u32[]{:S(2)}, u32[]{:S(2)}) collective-permute-start(bf16[264,1024]{1,0:T(8,128)(2,1)S(1)} %collective-permute-done.1), channel_id=1, source_target_pairs={{0,1},{4,12},{1,2},{5,4},{2,3},{6,5},{3,11},{7,6},{11,10},{15,7},{... | collective-permute-start | bytes 1622024 | tf_op jit(solution)/shard_map/ppermute | solution.py:303
  10.0 3.3 %collective-permute-done.refs_1_ = bf16[264,1024]{1,0:T(8,128)(2,1)S(1)} collective-permute-done((bf16[264,1024]{1,0:T(8,128)(2,1)}, bf16[264,1024]{1,0:T(8,128)(2,1)S(1)}, u32[]{:S(2)}, u32[]{:S(2)}) %collective-permute-start) | collective-permute-done | bytes 540704 | tf_op jit(solution)/shard_map/ppermute | solution.py:303
  13.2 2.1 %collective-permute-start.5 = (bf16[264,1024]{1,0:T(8,128)(2,1)S(1)}, bf16[264,1024]{1,0:T(8,128)(2,1)S(1)}, u32[]{:S(2)}, u32[]{:S(2)}) collective-permute-start(bf16[264,1024]{1,0:T(8,128)(2,1)S(1)} %collective-permute-done.refs_1_), channel_id=1, source_target_pairs={{0,1},{4,12},{1,2},{5,4},{2,3},{6,5},{3,11},{7,6},{11,10},{15,7},{... | collective-permute-start | bytes 1622024 | tf_op jit(solution)/shard_map/ppermute | solution.py:303
  15.4 3.6 %collective-permute-done.2.refs_2_ = bf16[264,1024]{1,0:T(8,128)(2,1)S(1)} collective-permute-done((bf16[264,1024]{1,0:T(8,128)(2,1)S(1)}, bf16[264,1024]{1,0:T(8,128)(2,1)S(1)}, u32[]{:S(2)}, u32[]{:S(2)}) %collective-permute-start.2) | collective-permute-done | bytes 540704 | tf_op jit(solution)/shard_map/ppermute | solution.py:303
  20.2 2.2 %collective-permute-start.7 = (bf16[264,1024]{1,0:T(8,128)(2,1)S(1)}, bf16[264,1024]{1,0:T(8,128)(2,1)S(1)}, u32[]{:S(2)}, u32[]{:S(2)}) collective-permute-start(bf16[264,1024]{1,0:T(8,128)(2,1)S(1)} %collective-permute-done.2.refs_2_), channel_id=1, source_target_pairs={{0,1},{4,12},{1,2},{5,4},{2,3},{6,5},{3,11},{7,6},{11,10},{15,7},{... | collective-permute-start | bytes 1622024 | tf_op jit(solution)/shard_map/ppermute | solution.py:303
  22.4 2.4 %collective-permute-done.5.refs_0_ = bf16[264,1024]{1,0:T(8,128)(2,1)S(1)} collective-permute-done((bf16[264,1024]{1,0:T(8,128)(2,1)S(1)}, bf16[264,1024]{1,0:T(8,128)(2,1)S(1)}, u32[]{:S(2)}, u32[]{:S(2)}) %collective-permute-start.5) | collective-permute-done | bytes 540704 | tf_op jit(solution)/shard_map/ppermute | solution.py:303
  24.8 2.1 %collective-permute-start.6 = (bf16[264,1024]{1,0:T(8,128)(2,1)S(1)}, bf16[264,1024]{1,0:T(8,128)(2,1)S(1)}, u32[]{:S(2)}, u32[]{:S(2)}) collective-permute-start(bf16[264,1024]{1,0:T(8,128)(2,1)S(1)} %collective-permute-done.5.refs_0_), channel_id=1, source_target_pairs={{0,1},{4,12},{1,2},{5,4},{2,3},{6,5},{3,11},{7,6},{11,10},{15,7},{... | collective-permute-start | bytes 1622024 | tf_op jit(solution)/shard_map/ppermute | solution.py:303
  26.9 3.7 %collective-permute-done.7.refs_1_ = bf16[264,1024]{1,0:T(8,128)(2,1)S(1)} collective-permute-done((bf16[264,1024]{1,0:T(8,128)(2,1)S(1)}, bf16[264,1024]{1,0:T(8,128)(2,1)S(1)}, u32[]{:S(2)}, u32[]{:S(2)}) %collective-permute-start.7) | collective-permute-done | bytes 540704 | tf_op jit(solution)/shard_map/ppermute | solution.py:303
  31.7 2.2 %collective-permute-start.8 = (bf16[264,1024]{1,0:T(8,128)(2,1)S(1)}, bf16[264,1024]{1,0:T(8,128)(2,1)S(1)}, u32[]{:S(2)}, u32[]{:S(2)}) collective-permute-start(bf16[264,1024]{1,0:T(8,128)(2,1)S(1)} %collective-permute-done.7.refs_1_), channel_id=1, source_target_pairs={{0,1},{4,12},{1,2},{5,4},{2,3},{6,5},{3,11},{7,6},{11,10},{15,7},{... | collective-permute-start | bytes 1622024 | tf_op jit(solution)/shard_map/ppermute | solution.py:303
  33.8 2.6 %collective-permute-done.6.refs_0_ = bf16[264,1024]{1,0:T(8,128)(2,1)S(1)} collective-permute-done((bf16[264,1024]{1,0:T(8,128)(2,1)S(1)}, bf16[264,1024]{1,0:T(8,128)(2,1)S(1)}, u32[]{:S(2)}, u32[]{:S(2)}) %collective-permute-start.6) | collective-permute-done | bytes 540704 | tf_op jit(solution)/shard_map/ppermute | solution.py:303
  36.4 2.1 %collective-permute-start.18 = (bf16[264,1024]{1,0:T(8,128)(2,1)S(1)}, bf16[264,1024]{1,0:T(8,128)(2,1)S(1)}, u32[]{:S(2)}, u32[]{:S(2)}) collective-permute-start(bf16[264,1024]{1,0:T(8,128)(2,1)S(1)} %collective-permute-done.6.refs_0_), channel_id=1, source_target_pairs={{0,1},{4,12},{1,2},{5,4},{2,3},{6,5},{3,11},{7,6},{11,10},{15,7},{... | collective-permute-start | bytes 1622024 | tf_op jit(solution)/shard_map/ppermute | solution.py:303
  38.5 2.6 %shard_map.96 = (bf16[192,1152]{1,0:T(8,128)(2,1)S(1)}, bf16[192,1152]{1,0:T(8,128)(2,1)S(1)}, bf16[384,1024]{1,0:T(8,128)(2,1)S(1)}, bf16[384,384]{1,0:T(8,128)...) custom-call(s32[2]{0:T(128)S(1)} %pad_add_fusion.ids_ref, ...), custom_call_target="tpu_custom_call" | custom-call | flops 15099494400 | bytes 1048576 | tf_op jit(solution)/shard_map/pallas_call | solution.py:274
  43.3 1.9 %shard_map.102 = (bf16[128,1152]{1,0:T(8,128)(2,1)S(1)}, bf16[128,1152]{1,0:T(8,128)(2,1)S(1)}, bf16[256,1024]{1,0:T(8,128)(2,1)S(1)}, bf16[256,384]{1,0:T(8,128...) custom-call(s32[2]{0:T(128)S(1)} %pad_add_fusion.ids_ref, ...), custom_call_target="tpu_custom_call" | custom-call | flops 10066329600 | bytes 1048576 | tf_op jit(solution)/shard_map/pallas_call | solution.py:274
  46.1 1.9 %shard_map.99 = (bf16[128,1152]{1,0:T(8,128)(2,1)S(1)}, bf16[128,1152]{1,0:T(8,128)(2,1)S(1)}, bf16[256,1024]{1,0:T(8,128)(2,1)S(1)}, bf16[256,384]{1,0:T(8,128)...) custom-call(s32[2]{0:T(128)S(1)} %pad_add_fusion.ids_ref, ...), custom_call_target="tpu_custom_call" | custom-call | flops 10066329600 | bytes 1048576 | tf_op jit(solution)/shard_map/pallas_call | solution.py:274
  50.2 2.1 %collective-permute-start.11 = (bf16[136,1024]{1,0:T(8,128)(2,1)S(1)}, bf16[136,1024]{1,0:T(8,128)(2,1)S(1)}, u32[]{:S(2)}, u32[]{:S(2)}) collective-permute-start(bf16[136,1024]{1,0:T(8,128)(2,1)S(1)} %get-tuple-element.78), channel_id=1, source_target_pairs={{0,8},{4,5},{1,0},{5,6},{2,1},{6,7},{3,2},{7,15},{11,3},{15,14},{1... | collective-permute-start | bytes 835592 | tf_op jit(solution)/shard_map/ppermute | solution.py:303
  53.8 1.6 %collective-permute-start.17 = (bf16[136,1024]{1,0:T(8,128)(2,1)S(1)}, bf16[136,1024]{1,0:T(8,128)(2,1)S(1)}, u32[]{:S(2)}, u32[]{:S(2)}) collective-permute-start(bf16[136,1024]{1,0:T(8,128)(2,1)S(1)} %get-tuple-element.87), channel_id=1, source_target_pairs={{0,8},{4,5},{1,0},{5,6},{2,1},{6,7},{3,2},{7,15},{11,3},{15,14},{1... | collective-permute-start | bytes 835592 | tf_op jit(solution)/shard_map/ppermute | solution.py:303
  55.7 2.6 %collective-permute-start.21 = (bf16[136,1024]{1,0:T(8,128)(2,1)S(1)}, bf16[136,1024]{1,0:T(8,128)(2,1)S(1)}, u32[]{:S(2)}, u32[]{:S(2)}) collective-permute-start(bf16[136,1024]{1,0:T(8,128)(2,1)S(1)} %shard_map.106), channel_id=1, source_target_pairs={{0,9},{4,6},{1,8},{5,7},{2,0},{6,15},{3,1},{7,14},{11,2},{15,13},{... | collective-permute-start | bytes 835592 | tf_op jit(solution)/shard_map/ppermute | solution.py:303
  60.4 5.1 %collective-permute-done.21 = bf16[136,1024]{1,0:T(8,128)(2,1)S(1)} collective-permute-done((bf16[136,1024]{1,0:T(8,128)(2,1)S(1)}, bf16[136,1024]{1,0:T(8,128)(2,1)S(1)}, u32[]{:S(2)}, u32[]{:S(2)}) %collective-permute-start.21) | collective-permute-done | bytes 278560 | tf_op jit(solution)/shard_map/ppermute | solution.py:303
  65.6 2.5 %collective-permute-start.22 = (bf16[136,1024]{1,0:T(8,128)(2,1)S(1)}, bf16[136,1024]{1,0:T(8,128)(2,1)S(1)}, u32[]{:S(2)}, u32[]{:S(2)}) collective-permute-start(bf16[136,1024]{1,0:T(8,128)(2,1)S(1)} %add_convert_fusion.1), channel_id=1, source_target_pairs={{0,8},{4,5},{1,0},{5,6},{2,1},{6,7},{3,2},{7,15},{11,3},{15,14},{1... | collective-permute-start | bytes 835592 | tf_op jit(solution)/shard_map/ppermute | solution.py:303
  70.4 2.0 %shard_map.108 = (f32[1024,768]{1,0:T(8,128)S(1)}, f32[384,1024]{1,0:T(8,128)S(1)}) custom-call(bf16[384,1024]{1,0:T(8,128)(2,1)S(1)} %get-tuple-element.99.refs_0_, bf16[384,384]{1,0:T(8,128)(2,1)S(1)} %get-tuple-element.100.refs_1_, bf16[384,768]{1,0:T(8,128)(2,1)S(1)} %get-tuple-element.101.refs_2_, bf16[384,1024]{1,0:T(8,128)(2,1)S(1)} %get-tuple-element.102.refs_3_, ...), custom_call_target="tpu_custom_call" | custom-call | flops 15099494400 | bytes 1048576 | tf_op jit(solution)/shard_map/pallas_call | solution.py:274
  75.1 1.7 %collective-permute-done.15 = bf16[136,1024]{1,0:T(8,128)(2,1)S(1)} collective-permute-done((bf16[136,1024]{1,0:T(8,128)(2,1)S(1)}, bf16[136,1024]{1,0:T(8,128)(2,1)S(1)}, u32[]{:S(2)}, u32[]{:S(2)}) %collective-permute-start.15) | collective-permute-done | bytes 278560 | tf_op jit(solution)/shard_map/ppermute | solution.py:303
  76.7 2.9 %shard_map.109 = (bf16[1,1024,768]{2,1,0:T(8,128)(2,1)}, bf16[1,384,1024]{2,1,0:T(8,128)(2,1)}) custom-call(f32[1024,768]{1,0:T(8,128)S(1)} %get-tuple-element.107.refs_0_, f32[384,1024]{1,0:T(8,128)S(1)} %get-tuple-element.108.refs_1_, bf16[256,1024]{1,0:T(8,128)(2,1)S(1)} %get-tuple-element.90.refs_2_, bf16[256,384]{1,0:T(8,128)(2,1)S(1)} %get-tuple-element.109.refs_3_, ...), custom_call_target="tpu_custom_call" | custom-call | flops 9059696640 | bytes 1048576 | tf_op jit(solution)/shard_map/pallas_call | solution.py:274
  (56 shorter events, 20.6 us)
Async XLA Ops:
  2.6 3.2 %collective-permute-start.1 = (bf16[264,1024]{1,0:T(8,128)(2,1)}, bf16[264,1024]{1,0:T(8,128)(2,1)S(1)}, u32[]{:S(2)}, u32[]{:S(2)}) collective-permute-start(bf16[264,1024]{1,0:T(8,128)(2,1)} %shard_map.93.refs_0_), channel_id=1, source_target_pairs={{0,4},{4,0},{1,5},{5,1},{2,6},{6,2},{3,7},{7,3},{11,15},{15,11},{1... | collective-permute-start | bytes 1622024 | tf_op jit(solution)/shard_map/ppermute | solution.py:307
  3.1 10.1 %collective-permute-start = (bf16[264,1024]{1,0:T(8,128)(2,1)}, bf16[264,1024]{1,0:T(8,128)(2,1)S(1)}, u32[]{:S(2)}, u32[]{:S(2)}) collective-permute-start(bf16[264,1024]{1,0:T(8,128)(2,1)} %shard_map.93.refs_0_), channel_id=1, source_target_pairs={{0,1},{4,12},{1,2},{5,4},{2,3},{6,5},{3,11},{7,6},{11,10},{15,7},{... | collective-permute-start | bytes 1622024 | tf_op jit(solution)/shard_map/ppermute | solution.py:303
  5.8 13.3 %collective-permute-start.2 = (bf16[264,1024]{1,0:T(8,128)(2,1)S(1)}, bf16[264,1024]{1,0:T(8,128)(2,1)S(1)}, u32[]{:S(2)}, u32[]{:S(2)}) collective-permute-start(bf16[264,1024]{1,0:T(8,128)(2,1)S(1)} %collective-permute-done.1), channel_id=1, source_target_pairs={{0,1},{4,12},{1,2},{5,4},{2,3},{6,5},{3,11},{7,6},{11,10},{15,7},{... | collective-permute-start | bytes 1622024 | tf_op jit(solution)/shard_map/ppermute | solution.py:303
  13.2 11.6 %collective-permute-start.5 = (bf16[264,1024]{1,0:T(8,128)(2,1)S(1)}, bf16[264,1024]{1,0:T(8,128)(2,1)S(1)}, u32[]{:S(2)}, u32[]{:S(2)}) collective-permute-start(bf16[264,1024]{1,0:T(8,128)(2,1)S(1)} %collective-permute-done.refs_1_), channel_id=1, source_target_pairs={{0,1},{4,12},{1,2},{5,4},{2,3},{6,5},{3,11},{7,6},{11,10},{15,7},{... | collective-permute-start | bytes 1622024 | tf_op jit(solution)/shard_map/ppermute | solution.py:303
  20.1 18.4 %collective-permute-start.3 = (bf16[192,2176]{1,0:T(8,128)(2,1)S(1)}, bf16[192,2176]{1,0:T(8,128)(2,1)S(1)}, u32[]{:S(2)}, u32[]{:S(2)}) collective-permute-start(bf16[192,2176]{1,0:T(8,128)(2,1)S(1)} %get-tuple-element.65), channel_id=1, source_target_pairs={{0,4},{4,0},{1,5},{5,1},{2,6},{6,2},{3,7},{7,3},{11,15},{15,11},{1... | collective-permute-start | bytes 2506760 | tf_op jit(solution)/shard_map/ppermute | solution.py:307
  20.2 10.4 %collective-permute-start.7 = (bf16[264,1024]{1,0:T(8,128)(2,1)S(1)}, bf16[264,1024]{1,0:T(8,128)(2,1)S(1)}, u32[]{:S(2)}, u32[]{:S(2)}) collective-permute-start(bf16[264,1024]{1,0:T(8,128)(2,1)S(1)} %collective-permute-done.2.refs_2_), channel_id=1, source_target_pairs={{0,1},{4,12},{1,2},{5,4},{2,3},{6,5},{3,11},{7,6},{11,10},{15,7},{... | collective-permute-start | bytes 1622024 | tf_op jit(solution)/shard_map/ppermute | solution.py:303
  24.8 11.6 %collective-permute-start.6 = (bf16[264,1024]{1,0:T(8,128)(2,1)S(1)}, bf16[264,1024]{1,0:T(8,128)(2,1)S(1)}, u32[]{:S(2)}, u32[]{:S(2)}) collective-permute-start(bf16[264,1024]{1,0:T(8,128)(2,1)S(1)} %collective-permute-done.5.refs_0_), channel_id=1, source_target_pairs={{0,1},{4,12},{1,2},{5,4},{2,3},{6,5},{3,11},{7,6},{11,10},{15,7},{... | collective-permute-start | bytes 1622024 | tf_op jit(solution)/shard_map/ppermute | solution.py:303
  31.6 11.7 %collective-permute-start.12 = (bf16[128,2176]{1,0:T(8,128)(2,1)S(1)}, bf16[128,2176]{1,0:T(8,128)(2,1)S(1)}, u32[]{:S(2)}, u32[]{:S(2)}) collective-permute-start(bf16[128,2176]{1,0:T(8,128)(2,1)S(1)} %get-tuple-element.80), channel_id=1, source_target_pairs={{0,4},{4,0},{1,5},{5,1},{2,6},{6,2},{3,7},{7,3},{11,15},{15,11},{1... | collective-permute-start | bytes 1671176 | tf_op jit(solution)/shard_map/ppermute | solution.py:307
  31.7 10.5 %collective-permute-start.8 = (bf16[264,1024]{1,0:T(8,128)(2,1)S(1)}, bf16[264,1024]{1,0:T(8,128)(2,1)S(1)}, u32[]{:S(2)}, u32[]{:S(2)}) collective-permute-start(bf16[264,1024]{1,0:T(8,128)(2,1)S(1)} %collective-permute-done.7.refs_1_), channel_id=1, source_target_pairs={{0,1},{4,12},{1,2},{5,4},{2,3},{6,5},{3,11},{7,6},{11,10},{15,7},{... | collective-permute-start | bytes 1622024 | tf_op jit(solution)/shard_map/ppermute | solution.py:303
  36.4 12.1 %collective-permute-start.18 = (bf16[264,1024]{1,0:T(8,128)(2,1)S(1)}, bf16[264,1024]{1,0:T(8,128)(2,1)S(1)}, u32[]{:S(2)}, u32[]{:S(2)}) collective-permute-start(bf16[264,1024]{1,0:T(8,128)(2,1)S(1)} %collective-permute-done.6.refs_0_), channel_id=1, source_target_pairs={{0,1},{4,12},{1,2},{5,4},{2,3},{6,5},{3,11},{7,6},{11,10},{15,7},{... | collective-permute-start | bytes 1622024 | tf_op jit(solution)/shard_map/ppermute | solution.py:303
  41.1 4.6 %collective-permute-start.4 = (bf16[192,1152]{1,0:T(8,128)(2,1)S(1)}, bf16[192,1152]{1,0:T(8,128)(2,1)S(1)}, u32[]{:S(2)}, u32[]{:S(2)}) collective-permute-start(bf16[192,1152]{1,0:T(8,128)(2,1)S(1)} %get-tuple-element.67), channel_id=1, source_target_pairs={{0,4},{4,0},{1,5},{5,1},{2,6},{6,2},{3,7},{7,3},{11,15},{15,11},{1... | collective-permute-start | bytes 1327112 | tf_op jit(solution)/shard_map/ppermute | solution.py:307
  43.2 3.0 %collective-permute-start.9 = (bf16[128,2176]{1,0:T(8,128)(2,1)S(1)}, bf16[128,2176]{1,0:T(8,128)(2,1)S(1)}, u32[]{:S(2)}, u32[]{:S(2)}) collective-permute-start(bf16[128,2176]{1,0:T(8,128)(2,1)S(1)} %get-tuple-element.73), channel_id=1, source_target_pairs={{0,4},{4,0},{1,5},{5,1},{2,6},{6,2},{3,7},{7,3},{11,15},{15,11},{1... | collective-permute-start | bytes 1671176 | tf_op jit(solution)/shard_map/ppermute | solution.py:307
  45.2 3.0 %collective-permute-start.13 = (bf16[128,1152]{1,0:T(8,128)(2,1)S(1)}, bf16[128,1152]{1,0:T(8,128)(2,1)S(1)}, u32[]{:S(2)}, u32[]{:S(2)}) collective-permute-start(bf16[128,1152]{1,0:T(8,128)(2,1)S(1)} %get-tuple-element.82), channel_id=1, source_target_pairs={{0,4},{4,0},{1,5},{5,1},{2,6},{6,2},{3,7},{7,3},{11,15},{15,11},{1... | collective-permute-start | bytes 884744 | tf_op jit(solution)/shard_map/ppermute | solution.py:307
  48.1 1.8 %collective-permute-start.10 = (bf16[128,1152]{1,0:T(8,128)(2,1)S(1)}, bf16[128,1152]{1,0:T(8,128)(2,1)S(1)}, u32[]{:S(2)}, u32[]{:S(2)}) collective-permute-start(bf16[128,1152]{1,0:T(8,128)(2,1)S(1)} %get-tuple-element.75), channel_id=1, source_target_pairs={{0,4},{4,0},{1,5},{5,1},{2,6},{6,2},{3,7},{7,3},{11,15},{15,11},{1... | collective-permute-start | bytes 884744 | tf_op jit(solution)/shard_map/ppermute | solution.py:307
  49.3 3.0 %collective-permute-start.19 = (bf16[64,2176]{1,0:T(8,128)(2,1)S(1)}, bf16[64,2176]{1,0:T(8,128)(2,1)S(1)}, u32[]{:S(2)}, u32[]{:S(2)}) collective-permute-start(bf16[64,2176]{1,0:T(8,128)(2,1)S(1)} %get-tuple-element.93), channel_id=1, source_target_pairs={{0,4},{4,0},{1,5},{5,1},{2,6},{6,2},{3,7},{7,3},{11,15},{15,11},{1... | collective-permute-start | bytes 835592 | tf_op jit(solution)/shard_map/ppermute | solution.py:307
  50.2 8.1 %collective-permute-start.11 = (bf16[136,1024]{1,0:T(8,128)(2,1)S(1)}, bf16[136,1024]{1,0:T(8,128)(2,1)S(1)}, u32[]{:S(2)}, u32[]{:S(2)}) collective-permute-start(bf16[136,1024]{1,0:T(8,128)(2,1)S(1)} %get-tuple-element.78), channel_id=1, source_target_pairs={{0,8},{4,5},{1,0},{5,6},{2,1},{6,7},{3,2},{7,15},{11,3},{15,14},{1... | collective-permute-start | bytes 835592 | tf_op jit(solution)/shard_map/ppermute | solution.py:303
  53.7 1.7 %collective-permute-start.20 = (bf16[64,1152]{1,0:T(8,128)(2,1)S(1)}, bf16[64,1152]{1,0:T(8,128)(2,1)S(1)}, u32[]{:S(2)}, u32[]{:S(2)}) collective-permute-start(bf16[64,1152]{1,0:T(8,128)(2,1)S(1)} %get-tuple-element.95), channel_id=1, source_target_pairs={{0,4},{4,0},{1,5},{5,1},{2,6},{6,2},{3,7},{7,3},{11,15},{15,11},{1... | collective-permute-start | bytes 442376 | tf_op jit(solution)/shard_map/ppermute | solution.py:307
  53.8 6.6 %collective-permute-start.17 = (bf16[136,1024]{1,0:T(8,128)(2,1)S(1)}, bf16[136,1024]{1,0:T(8,128)(2,1)S(1)}, u32[]{:S(2)}, u32[]{:S(2)}) collective-permute-start(bf16[136,1024]{1,0:T(8,128)(2,1)S(1)} %get-tuple-element.87), channel_id=1, source_target_pairs={{0,8},{4,5},{1,0},{5,6},{2,1},{6,7},{3,2},{7,15},{11,3},{15,14},{1... | collective-permute-start | bytes 835592 | tf_op jit(solution)/shard_map/ppermute | solution.py:303
  55.7 9.8 %collective-permute-start.21 = (bf16[136,1024]{1,0:T(8,128)(2,1)S(1)}, bf16[136,1024]{1,0:T(8,128)(2,1)S(1)}, u32[]{:S(2)}, u32[]{:S(2)}) collective-permute-start(bf16[136,1024]{1,0:T(8,128)(2,1)S(1)} %shard_map.106), channel_id=1, source_target_pairs={{0,9},{4,6},{1,8},{5,7},{2,0},{6,15},{3,1},{7,14},{11,2},{15,13},{... | collective-permute-start | bytes 835592 | tf_op jit(solution)/shard_map/ppermute | solution.py:303
  58.4 11.0 %collective-permute-start.14 = (bf16[136,1024]{1,0:T(8,128)(2,1)S(1)}, bf16[136,1024]{1,0:T(8,128)(2,1)S(1)}, u32[]{:S(2)}, u32[]{:S(2)}) collective-permute-start(bf16[136,1024]{1,0:T(8,128)(2,1)S(1)} %add_convert_fusion.3), channel_id=1, source_target_pairs={{0,8},{4,5},{1,0},{5,6},{2,1},{6,7},{3,2},{7,15},{11,3},{15,14},{1... | collective-permute-start | bytes 835592 | tf_op jit(solution)/shard_map/ppermute | solution.py:303
  65.6 8.1 %collective-permute-start.22 = (bf16[136,1024]{1,0:T(8,128)(2,1)S(1)}, bf16[136,1024]{1,0:T(8,128)(2,1)S(1)}, u32[]{:S(2)}, u32[]{:S(2)}) collective-permute-start(bf16[136,1024]{1,0:T(8,128)(2,1)S(1)} %add_convert_fusion.1), channel_id=1, source_target_pairs={{0,8},{4,5},{1,0},{5,6},{2,1},{6,7},{3,2},{7,15},{11,3},{15,14},{1... | collective-permute-start | bytes 835592 | tf_op jit(solution)/shard_map/ppermute | solution.py:303
  69.5 7.2 %collective-permute-start.15 = (bf16[136,1024]{1,0:T(8,128)(2,1)S(1)}, bf16[136,1024]{1,0:T(8,128)(2,1)S(1)}, u32[]{:S(2)}, u32[]{:S(2)}) collective-permute-start(bf16[136,1024]{1,0:T(8,128)(2,1)S(1)} %add_convert_fusion.2), channel_id=1, source_target_pairs={{0,8},{4,5},{1,0},{5,6},{2,1},{6,7},{3,2},{7,15},{11,3},{15,14},{1... | collective-permute-start | bytes 835592 | tf_op jit(solution)/shard_map/ppermute | solution.py:303
  73.8 6.6 %collective-permute-start.23 = (bf16[136,1024]{1,0:T(8,128)(2,1)S(1)}, bf16[136,1024]{1,0:T(8,128)(2,1)S(1)}, u32[]{:S(2)}, u32[]{:S(2)}) collective-permute-start(bf16[136,1024]{1,0:T(8,128)(2,1)S(1)} %add_convert_fusion), channel_id=1, source_target_pairs={{0,8},{4,5},{1,0},{5,6},{2,1},{6,7},{3,2},{7,15},{11,3},{15,14},{1... | collective-permute-start | bytes 835592 | tf_op jit(solution)/shard_map/ppermute | solution.py:303
  76.7 3.7 %collective-permute-start.16 = (bf16[136,1024]{1,0:T(8,128)(2,1)S(1)}, bf16[136,1024]{1,0:T(8,128)(2,1)S(1)}, u32[]{:S(2)}, u32[]{:S(2)}) collective-permute-start(bf16[136,1024]{1,0:T(8,128)(2,1)S(1)} %collective-permute-done.15), channel_id=1, source_target_pairs={{0,4},{4,0},{1,5},{5,1},{2,6},{6,2},{3,7},{7,3},{11,15},{15,11},{1... | collective-permute-start | bytes 835592 | tf_op jit(solution)/shard_map/ppermute | solution.py:307
  (5 other events, 40.5 us)
